TPU v7x, 32 devices: a whole 2x2x4 slice. The times are simulated.
32 devices in a mesh: dp: 2 (over y), row: 2 (over x), col: 8 (over z, core).
Axes of the slice: x: 2, y: 2, z: 4, core: 2. Of those that a mesh axis runs over, the one named last changes fastest.
Arguments:
- view_a: bfloat16 [256, 32768], P('dp', ('row', 'col')), may hold values from -22 to 22
- view_b: bfloat16 [256, 32768], P('dp', ('row', 'col')), may hold values from -22 to 22
Outputs:
- grad_a: float32 [256, 32768], P('dp', ('row', 'col'))
- grad_b: float32 [256, 32768], P('dp', ('row', 'col'))
- objective: float32 [], replicated
All inputs are finite; a program needn't handle non-finite values.
Results may differ from a plain program's by a relative error of at most 0.0028.
Values may be sent and summed in bfloat16 or wider, within the bound.
A program may use at most 64 MiB of HBM per device.

v0:
```python
import jax
import jax.numpy as jnp
from jax import lax
from jax.sharding import PartitionSpec as P


def statistics(values, total):
    floats = values.astype(jnp.float32)
    mean = jnp.sum(floats, axis=0) / total
    diff = floats - mean
    std = jnp.sqrt(jnp.sum(diff * diff, axis=0) / (total - 1) + 0.0001)
    return (mean, std, diff.astype(jnp.bfloat16))


def on_device(view_a, view_b):
    n_dp = lax.axis_size("dp")
    n_row = lax.axis_size("row")
    n_col = lax.axis_size("col")
    dp_index = lax.axis_index("dp")
    row_index = lax.axis_index("row")
    col_index = lax.axis_index("col")
    n_dev, shard = view_a.shape
    total = n_dev * n_dp
    f_all = shard * n_row * n_col
    coef = 2.0 * total / (25.0 * (total - 1))
    row_width = shard * n_col // n_dp
    col_width = shard * n_row
    row_start = (row_index * n_col + dp_index * (n_col // n_dp)) * shard
    full_a, full_b = (
        lax.all_gather(view_a, "dp", axis=0, tiled=True),
        lax.all_gather(view_b, "dp", axis=0, tiled=True),
    )
    mean_a, std_a, cent_a = statistics(full_a, total)
    mean_b, std_b, cent_b = statistics(full_b, total)
    wide_a, wide_b = (
        lax.all_gather(cent_a, "col", axis=1, tiled=True),
        lax.all_gather(cent_b, "col", axis=1, tiled=True),
    )
    rows_a = lax.dynamic_slice_in_dim(wide_a, dp_index * row_width, row_width, 1)
    rows_b = lax.dynamic_slice_in_dim(wide_b, dp_index * row_width, row_width, 1)
    cols_a, cols_b = (
        lax.all_gather(cent_a, "row", axis=1, tiled=True),
        lax.all_gather(cent_b, "row", axis=1, tiled=True),
    )
    block = min(512, row_width)
    column_iota = jnp.arange(col_width, dtype=jnp.int32)
    col_ids = column_iota // shard * (n_col * shard) + col_index * shard + column_iota % shard

    def tile_part(rows, cols, start):
        strip = lax.dynamic_slice_in_dim(rows, start, block, 1)
        cov = lax.dot_general(
            strip, cols, (((0,), (0,)), ((), ())), preferred_element_type=jnp.float32
        ) / (total - 1)
        row_ids = row_start + start + jnp.arange(block, dtype=jnp.int32)
        off = jnp.where(row_ids[:, None] == col_ids[None, :], jnp.float32(0.0), cov)
        contrib = jnp.dot(
            strip.astype(jnp.float32),
            off,
            preferred_element_type=jnp.float32,
            precision=lax.Precision.HIGHEST,
        )
        return (contrib, jnp.sum(off * off))

    def one_block(index, carry):
        pull_a, pull_b, square = carry
        start = index * block
        contrib_a, square_a = tile_part(rows_a, cols_a, start)
        contrib_b, square_b = tile_part(rows_b, cols_b, start)
        return (pull_a + contrib_a, pull_b + contrib_b, square + square_a + square_b)

    zeros_pull = jnp.zeros((total, col_width), jnp.float32)
    pull_a, pull_b, square = lax.fori_loop(
        0, row_width // block, one_block, (zeros_pull, zeros_pull, jnp.zeros((), jnp.float32))
    )

    def arrange(pull):
        term = coef * (pull - jnp.sum(pull, axis=0) / total)
        term = term.reshape(n_dp, n_dev, n_row, shard).transpose(0, 2, 1, 3)
        return term.reshape(n_dp * n_row * n_dev, shard)

    back_a, back_b = (
        lax.psum_scatter(arrange(pull_a), ("dp", "row"), scatter_dimension=0, tiled=True),
        lax.psum_scatter(arrange(pull_b), ("dp", "row"), scatter_dimension=0, tiled=True),
    )
    own_a = view_a.astype(jnp.float32)
    own_b = view_b.astype(jnp.float32)
    gap = own_a - own_b
    hinge_a = jnp.where(
        std_a < 1.0, total * (own_a - mean_a) / (2.0 * std_a * (total - 1)), jnp.float32(0.0)
    )
    hinge_b = jnp.where(
        std_b < 1.0, total * (own_b - mean_b) / (2.0 * std_b * (total - 1)), jnp.float32(0.0)
    )
    grad_a = gap - hinge_a + back_a
    grad_b = -gap - hinge_b + back_b
    partial_loss = 25.0 * jnp.sum(gap * gap) / (total * f_all)
    partial_loss = partial_loss + 25.0 * (
        jnp.sum(jnp.maximum(1.0 - std_a, 0.0)) + jnp.sum(jnp.maximum(1.0 - std_b, 0.0))
    ) / (f_all * n_dp)
    partial_loss = partial_loss + square / f_all
    summed = lax.psum(partial_loss, ("dp", "row", "col"))
    objective = summed * total / (50.0 * f_all)
    return (grad_a, grad_b, objective)


def solution(mesh):
    in_specs = (P("dp", ("row", "col")), P("dp", ("row", "col")))
    out_specs = (P("dp", ("row", "col")), P("dp", ("row", "col")), P())
    return jax.shard_map(
        on_device, mesh=mesh, in_specs=in_specs, out_specs=out_specs, check_vma=False
    )
```

profile of v0, /device:TPU:0, one launch (start us, length us, event | category | flops | bytes accessed | tf_op | source)
XLA Modules:
  0.0 1034.7 jit_solution(6068727246909488327)
XLA Ops:
  8.7 24.9 %all-gather.7.cloned.1.call-done = bf16[256,2048]{1,0:T(8,128)(2,1)} async-done(((bf16[128,2048]{1,0:T(8,128)(2,1)}), bf16[256,2048]{1,0:T(8,128)(2,1)}) %all-gather.7.cloned.1.call-update) | async-done | bytes 1048592 | tf_op jit(solution)/shard_map/all_gather | solution.py:30
  37.6 18.9 %all-gather.13.cloned.1.call-done = bf16[256,2048]{1,0:T(8,128)(2,1)} async-done(((bf16[128,2048]{1,0:T(8,128)(2,1)}), bf16[256,2048]{1,0:T(8,128)(2,1)}) %all-gather.13.cloned.1.call-update) | async-done | bytes 1048592 | tf_op jit(solution)/shard_map/all_gather | solution.py:31
  61.6 79.1 %all-gather.9.cloned.1.call-done = bf16[256,16384]{1,0:T(8,128)(2,1)} async-done(((bf16[256,2048]{1,0:T(8,128)(2,1)}), bf16[256,16384]{1,0:T(8,128)(2,1)}) %all-gather.9.cloned.1.call-update) | async-done | bytes 8388624 | tf_op jit(solution)/shard_map/all_gather | solution.py:36
  145.3 78.1 %all-gather.15.cloned.1.call-done = bf16[256,16384]{1,0:T(8,128)(2,1)} async-done(((bf16[256,2048]{1,0:T(8,128)(2,1)}), bf16[256,16384]{1,0:T(8,128)(2,1)}) %all-gather.15.cloned.1.call-update) | async-done | bytes 8388624 | tf_op jit(solution)/shard_map/all_gather | solution.py:37
  228.0 29.1 %all-gather.11.cloned.1.call-done = bf16[256,4096]{1,0:T(8,128)(2,1)} async-done(((bf16[256,2048]{1,0:T(8,128)(2,1)}), bf16[256,4096]{1,0:T(8,128)(2,1)}) %all-gather.11.cloned.1.call-update) | async-done | bytes 2097168 | tf_op jit(solution)/shard_map/all_gather | solution.py:42
  257.0 35.1 %all-gather.17.cloned.1.call-done = bf16[256,4096]{1,0:T(8,128)(2,1)} async-done(((bf16[256,2048]{1,0:T(8,128)(2,1)}), bf16[256,4096]{1,0:T(8,128)(2,1)}) %all-gather.17.cloned.1.call-update) | async-done | bytes 2097168 | tf_op jit(solution)/shard_map/all_gather | solution.py:43
  292.2 554.5 %while.18 = (s32[]{:T(128)}, f32[256,4096]{1,0:T(8,128)}, f32[256,4096]{1,0:T(8,128)}, f32[]{:T(128)}, bf16[256,8192]{1,0:T(8,128)(2,1)}, /*index=5*/s32[]{:T(12...) while((s32[]{:T(128)}, f32[256,4096]{1,0:T(8,128)}, ...), condition=%wide.region_6.7_spmd.clone, body=%wide.region_3.6_spmd.clone.sunk | while | flops 15068098560 | bytes 139534720 | solution.py:72
  292.2 6.3 fusion.74
  298.5 11.1 %fusion.76 = f32[256,4096]{1,0:T(8,128)} fusion(f32[512,4096]{1,0:T(8,128)} %fusion.74, f32[256,4096]{1,0:T(8,128)} %get-tuple-element.331, s32[4096]{0:T(1024)S(1)} %fusion.75, s32[512]{0:T(512)S(1)} %iota_add_fusion.2, pred[]{:T(512)S(6)} %compare.6, bf16[256,8192]{1,0:T(8,128)(2,1)} %get-tuple-element.348, s32[]{:T(128)S(6)} %select_n.105), kind=kOutput, calls=%fused_computation.8.clone.1 | convolution fusion | flops 6450839552 | bytes 17057796 | tf_op jit(solution)/shard_map/while/body/eval_jaxpr/dot_general | solution.py:56
  309.6 5.3 multiply_reduce_fusion.4
  315.0 7.4 fusion.77
  325.7 6.3 fusion.74
  332.0 12.3 %fusion.76 = f32[256,4096]{1,0:T(8,128)} fusion(f32[512,4096]{1,0:T(8,128)} %fusion.74, f32[256,4096]{1,0:T(8,128)} %get-tuple-element.331, s32[4096]{0:T(1024)S(1)} %fusion.75, s32[512]{0:T(512)S(1)} %iota_add_fusion.2, pred[]{:T(512)S(6)} %compare.6, bf16[256,8192]{1,0:T(8,128)(2,1)} %get-tuple-element.348, s32[]{:T(128)S(6)} %select_n.105), kind=kOutput, calls=%fused_computation.8.clone.1 | convolution fusion | flops 6450839552 | bytes 17057796 | tf_op jit(solution)/shard_map/while/body/eval_jaxpr/dot_general | solution.py:56
  349.7 7.4 fusion.77
  360.4 6.3 fusion.74
  366.7 12.3 %fusion.76 = f32[256,4096]{1,0:T(8,128)} fusion(f32[512,4096]{1,0:T(8,128)} %fusion.74, f32[256,4096]{1,0:T(8,128)} %get-tuple-element.331, s32[4096]{0:T(1024)S(1)} %fusion.75, s32[512]{0:T(512)S(1)} %iota_add_fusion.2, pred[]{:T(512)S(6)} %compare.6, bf16[256,8192]{1,0:T(8,128)(2,1)} %get-tuple-element.348, s32[]{:T(128)S(6)} %select_n.105), kind=kOutput, calls=%fused_computation.8.clone.1 | convolution fusion | flops 6450839552 | bytes 17057796 | tf_op jit(solution)/shard_map/while/body/eval_jaxpr/dot_general | solution.py:56
  384.4 7.4 fusion.77
  395.1 6.3 fusion.74
  401.4 12.3 %fusion.76 = f32[256,4096]{1,0:T(8,128)} fusion(f32[512,4096]{1,0:T(8,128)} %fusion.74, f32[256,4096]{1,0:T(8,128)} %get-tuple-element.331, s32[4096]{0:T(1024)S(1)} %fusion.75, s32[512]{0:T(512)S(1)} %iota_add_fusion.2, pred[]{:T(512)S(6)} %compare.6, bf16[256,8192]{1,0:T(8,128)(2,1)} %get-tuple-element.348, s32[]{:T(128)S(6)} %select_n.105), kind=kOutput, calls=%fused_computation.8.clone.1 | convolution fusion | flops 6450839552 | bytes 17057796 | tf_op jit(solution)/shard_map/while/body/eval_jaxpr/dot_general | solution.py:56
  419.1 7.4 fusion.77
  429.9 6.3 fusion.74
  436.2 12.3 %fusion.76 = f32[256,4096]{1,0:T(8,128)} fusion(f32[512,4096]{1,0:T(8,128)} %fusion.74, f32[256,4096]{1,0:T(8,128)} %get-tuple-element.331, s32[4096]{0:T(1024)S(1)} %fusion.75, s32[512]{0:T(512)S(1)} %iota_add_fusion.2, pred[]{:T(512)S(6)} %compare.6, bf16[256,8192]{1,0:T(8,128)(2,1)} %get-tuple-element.348, s32[]{:T(128)S(6)} %select_n.105), kind=kOutput, calls=%fused_computation.8.clone.1 | convolution fusion | flops 6450839552 | bytes 17057796 | tf_op jit(solution)/shard_map/while/body/eval_jaxpr/dot_general | solution.py:56
  453.8 7.4 fusion.77
  464.6 6.3 fusion.74
  470.9 12.3 %fusion.76 = f32[256,4096]{1,0:T(8,128)} fusion(f32[512,4096]{1,0:T(8,128)} %fusion.74, f32[256,4096]{1,0:T(8,128)} %get-tuple-element.331, s32[4096]{0:T(1024)S(1)} %fusion.75, s32[512]{0:T(512)S(1)} %iota_add_fusion.2, pred[]{:T(512)S(6)} %compare.6, bf16[256,8192]{1,0:T(8,128)(2,1)} %get-tuple-element.348, s32[]{:T(128)S(6)} %select_n.105), kind=kOutput, calls=%fused_computation.8.clone.1 | convolution fusion | flops 6450839552 | bytes 17057796 | tf_op jit(solution)/shard_map/while/body/eval_jaxpr/dot_general | solution.py:56
  488.6 7.4 fusion.77
  499.3 6.3 fusion.74
  505.6 12.3 %fusion.76 = f32[256,4096]{1,0:T(8,128)} fusion(f32[512,4096]{1,0:T(8,128)} %fusion.74, f32[256,4096]{1,0:T(8,128)} %get-tuple-element.331, s32[4096]{0:T(1024)S(1)} %fusion.75, s32[512]{0:T(512)S(1)} %iota_add_fusion.2, pred[]{:T(512)S(6)} %compare.6, bf16[256,8192]{1,0:T(8,128)(2,1)} %get-tuple-element.348, s32[]{:T(128)S(6)} %select_n.105), kind=kOutput, calls=%fused_computation.8.clone.1 | convolution fusion | flops 6450839552 | bytes 17057796 | tf_op jit(solution)/shard_map/while/body/eval_jaxpr/dot_general | solution.py:56
  523.3 7.4 fusion.77
  534.0 6.3 fusion.74
  540.3 12.3 %fusion.76 = f32[256,4096]{1,0:T(8,128)} fusion(f32[512,4096]{1,0:T(8,128)} %fusion.74, f32[256,4096]{1,0:T(8,128)} %get-tuple-element.331, s32[4096]{0:T(1024)S(1)} %fusion.75, s32[512]{0:T(512)S(1)} %iota_add_fusion.2, pred[]{:T(512)S(6)} %compare.6, bf16[256,8192]{1,0:T(8,128)(2,1)} %get-tuple-element.348, s32[]{:T(128)S(6)} %select_n.105), kind=kOutput, calls=%fused_computation.8.clone.1 | convolution fusion | flops 6450839552 | bytes 17057796 | tf_op jit(solution)/shard_map/while/body/eval_jaxpr/dot_general | solution.py:56
  558.0 7.4 fusion.77
  568.7 6.3 fusion.74
  575.0 12.3 %fusion.76 = f32[256,4096]{1,0:T(8,128)} fusion(f32[512,4096]{1,0:T(8,128)} %fusion.74, f32[256,4096]{1,0:T(8,128)} %get-tuple-element.331, s32[4096]{0:T(1024)S(1)} %fusion.75, s32[512]{0:T(512)S(1)} %iota_add_fusion.2, pred[]{:T(512)S(6)} %compare.6, bf16[256,8192]{1,0:T(8,128)(2,1)} %get-tuple-element.348, s32[]{:T(128)S(6)} %select_n.105), kind=kOutput, calls=%fused_computation.8.clone.1 | convolution fusion | flops 6450839552 | bytes 17057796 | tf_op jit(solution)/shard_map/while/body/eval_jaxpr/dot_general | solution.py:56
  592.7 7.4 fusion.77
  603.5 6.3 fusion.74
  609.8 12.3 %fusion.76 = f32[256,4096]{1,0:T(8,128)} fusion(f32[512,4096]{1,0:T(8,128)} %fusion.74, f32[256,4096]{1,0:T(8,128)} %get-tuple-element.331, s32[4096]{0:T(1024)S(1)} %fusion.75, s32[512]{0:T(512)S(1)} %iota_add_fusion.2, pred[]{:T(512)S(6)} %compare.6, bf16[256,8192]{1,0:T(8,128)(2,1)} %get-tuple-element.348, s32[]{:T(128)S(6)} %select_n.105), kind=kOutput, calls=%fused_computation.8.clone.1 | convolution fusion | flops 6450839552 | bytes 17057796 | tf_op jit(solution)/shard_map/while/body/eval_jaxpr/dot_general | solution.py:56
  627.4 7.4 fusion.77
  638.2 6.3 fusion.74
  644.5 12.3 %fusion.76 = f32[256,4096]{1,0:T(8,128)} fusion(f32[512,4096]{1,0:T(8,128)} %fusion.74, f32[256,4096]{1,0:T(8,128)} %get-tuple-element.331, s32[4096]{0:T(1024)S(1)} %fusion.75, s32[512]{0:T(512)S(1)} %iota_add_fusion.2, pred[]{:T(512)S(6)} %compare.6, bf16[256,8192]{1,0:T(8,128)(2,1)} %get-tuple-element.348, s32[]{:T(128)S(6)} %select_n.105), kind=kOutput, calls=%fused_computation.8.clone.1 | convolution fusion | flops 6450839552 | bytes 17057796 | tf_op jit(solution)/shard_map/while/body/eval_jaxpr/dot_general | solution.py:56
  662.2 7.4 fusion.77
  672.9 6.3 fusion.74
  679.2 12.3 %fusion.76 = f32[256,4096]{1,0:T(8,128)} fusion(f32[512,4096]{1,0:T(8,128)} %fusion.74, f32[256,4096]{1,0:T(8,128)} %get-tuple-element.331, s32[4096]{0:T(1024)S(1)} %fusion.75, s32[512]{0:T(512)S(1)} %iota_add_fusion.2, pred[]{:T(512)S(6)} %compare.6, bf16[256,8192]{1,0:T(8,128)(2,1)} %get-tuple-element.348, s32[]{:T(128)S(6)} %select_n.105), kind=kOutput, calls=%fused_computation.8.clone.1 | convolution fusion | flops 6450839552 | bytes 17057796 | tf_op jit(solution)/shard_map/while/body/eval_jaxpr/dot_general | solution.py:56
  696.9 7.4 fusion.77
  707.6 6.3 fusion.74
  713.9 12.3 %fusion.76 = f32[256,4096]{1,0:T(8,128)} fusion(f32[512,4096]{1,0:T(8,128)} %fusion.74, f32[256,4096]{1,0:T(8,128)} %get-tuple-element.331, s32[4096]{0:T(1024)S(1)} %fusion.75, s32[512]{0:T(512)S(1)} %iota_add_fusion.2, pred[]{:T(512)S(6)} %compare.6, bf16[256,8192]{1,0:T(8,128)(2,1)} %get-tuple-element.348, s32[]{:T(128)S(6)} %select_n.105), kind=kOutput, calls=%fused_computation.8.clone.1 | convolution fusion | flops 6450839552 | bytes 17057796 | tf_op jit(solution)/shard_map/while/body/eval_jaxpr/dot_general | solution.py:56
  731.6 7.4 fusion.77
  742.3 6.3 fusion.74
  748.6 12.3 %fusion.76 = f32[256,4096]{1,0:T(8,128)} fusion(f32[512,4096]{1,0:T(8,128)} %fusion.74, f32[256,4096]{1,0:T(8,128)} %get-tuple-element.331, s32[4096]{0:T(1024)S(1)} %fusion.75, s32[512]{0:T(512)S(1)} %iota_add_fusion.2, pred[]{:T(512)S(6)} %compare.6, bf16[256,8192]{1,0:T(8,128)(2,1)} %get-tuple-element.348, s32[]{:T(128)S(6)} %select_n.105), kind=kOutput, calls=%fused_computation.8.clone.1 | convolution fusion | flops 6450839552 | bytes 17057796 | tf_op jit(solution)/shard_map/while/body/eval_jaxpr/dot_general | solution.py:56
  766.3 7.4 fusion.77
  777.1 6.3 fusion.74
  783.4 12.3 %fusion.76 = f32[256,4096]{1,0:T(8,128)} fusion(f32[512,4096]{1,0:T(8,128)} %fusion.74, f32[256,4096]{1,0:T(8,128)} %get-tuple-element.331, s32[4096]{0:T(1024)S(1)} %fusion.75, s32[512]{0:T(512)S(1)} %iota_add_fusion.2, pred[]{:T(512)S(6)} %compare.6, bf16[256,8192]{1,0:T(8,128)(2,1)} %get-tuple-element.348, s32[]{:T(128)S(6)} %select_n.105), kind=kOutput, calls=%fused_computation.8.clone.1 | convolution fusion | flops 6450839552 | bytes 17057796 | tf_op jit(solution)/shard_map/while/body/eval_jaxpr/dot_general | solution.py:56
  801.0 7.4 fusion.77
  811.8 6.3 fusion.74
  818.1 12.3 %fusion.76 = f32[256,4096]{1,0:T(8,128)} fusion(f32[512,4096]{1,0:T(8,128)} %fusion.74, f32[256,4096]{1,0:T(8,128)} %get-tuple-element.331, s32[4096]{0:T(1024)S(1)} %fusion.75, s32[512]{0:T(512)S(1)} %iota_add_fusion.2, pred[]{:T(512)S(6)} %compare.6, bf16[256,8192]{1,0:T(8,128)(2,1)} %get-tuple-element.348, s32[]{:T(128)S(6)} %select_n.105), kind=kOutput, calls=%fused_computation.8.clone.1 | convolution fusion | flops 6450839552 | bytes 17057796 | tf_op jit(solution)/shard_map/while/body/eval_jaxpr/dot_general | solution.py:56
  835.8 7.4 fusion.77
  851.5 8.5 subtract_multiply_fusion
  860.0 6.6 reshape.49
  866.5 6.6 copy.6
  873.2 6.6 reshape.47
  879.8 6.7 copy.5
  889.1 36.9 %reduce-scatter.5.cloned.1.call-done = f32[128,2048]{1,0:T(8,128)} async-done(((f32[512,2048]{1,0:T(8,128)}), f32[128,2048]{1,0:T(8,128)}) %reduce-scatter.5.cloned.1.call-update) | async-done | bytes 1048592 | tf_op jit(solution)/shard_map/reduce_scatter | solution.py:83
  926.0 56.0 %reduce-scatter.3.cloned.1.call-done = f32[128,2048]{1,0:T(8,128)} async-done(((f32[512,2048]{1,0:T(8,128)}), f32[128,2048]{1,0:T(8,128)}) %reduce-scatter.3.cloned.1.call-update) | async-done | bytes 1048592 | tf_op jit(solution)/shard_map/reduce_scatter | solution.py:82
  986.7 39.4 %psum.7 = f32[]{:T(128)} all-reduce(f32[]{:T(128)S(6)} %add.148), channel_id=1, replica_groups=mesh['dp'=2,'row'=2,'col'=8] {'dp','row','col'}, use_global_device_ids=true, to_apply=%region_15.16 | all-reduce | flops 1 | bytes 8 | tf_op jit(solution)/shard_map/psum | solution.py:101
  (214 shorter events, 141.8 us)
Async XLA Ops:
  7.2 26.4 %all-gather.7.cloned.1.call-start = ((), (), s32[]{:S(2)}) async-start(), calls=%async_computation.2 | async-start | bytes 1572864 | tf_op jit(solution)/shard_map/all_gather | solution.py:30
  7.9 48.6 %all-gather.13.cloned.1.call-start = ((), (), s32[]{:S(2)}) async-start(), calls=%async_computation.5 | async-start | bytes 1572864 | tf_op jit(solution)/shard_map/all_gather | solution.py:31
  8.6 132.1 %all-gather.9.cloned.1.call-start = ((), (), s32[]{:S(2)}) async-start(), calls=%async_computation.3 | async-start | bytes 9437184 | tf_op jit(solution)/shard_map/all_gather | solution.py:36
  37.5 185.9 %all-gather.15.cloned.1.call-start = ((), (), s32[]{:S(2)}) async-start(), calls=%async_computation.6 | async-start | bytes 9437184 | tf_op jit(solution)/shard_map/all_gather | solution.py:37
  60.4 196.6 %all-gather.11.cloned.1.call-start = ((), (), s32[]{:S(2)}) async-start(), calls=%async_computation.4 | async-start | bytes 3145728 | tf_op jit(solution)/shard_map/all_gather | solution.py:42
  61.0 231.2 %all-gather.17.cloned.1.call-start = ((), (), s32[]{:S(2)}) async-start(), calls=%async_computation.7 | async-start | bytes 3145728 | tf_op jit(solution)/shard_map/all_gather | solution.py:43
  61.6 864.4 %reduce-scatter.5.cloned.1.call-start = ((), (), s32[]{:S(2)}) async-start(), calls=%async_computation.9 | async-start | bytes 5242880 | tf_op jit(solution)/shard_map/reduce_scatter | solution.py:83
  298.5 11.1 %copy-start = (f32[512,4096]{1,0:T(8,128)S(1)}, f32[512,4096]{1,0:T(8,128)}, u32[]{:S(2)}) copy-start(f32[512,4096]{1,0:T(8,128)} %fusion.74) | copy-start | bytes 25165828 | tf_op jit(solution)/shard_map/while
  298.5 11.1 %copy-start.5 = (bf16[256,4096]{1,0:T(8,128)(2,1)S(1)}, bf16[256,4096]{1,0:T(8,128)(2,1)}, u32[]{:S(2)}) copy-start(bf16[256,4096]{1,0:T(8,128)(2,1)} %get-tuple-element.352) | copy-start | bytes 6291460 | tf_op jit(solution)/shard_map/while
  309.6 5.4 copy-start.1
  322.4 2.0 copy-start.2
  332.0 12.3 %copy-start = (f32[512,4096]{1,0:T(8,128)S(1)}, f32[512,4096]{1,0:T(8,128)}, u32[]{:S(2)}) copy-start(f32[512,4096]{1,0:T(8,128)} %fusion.74) | copy-start | bytes 25165828 | tf_op jit(solution)/shard_map/while
  332.0 12.3 %copy-start.5 = (bf16[256,4096]{1,0:T(8,128)(2,1)S(1)}, bf16[256,4096]{1,0:T(8,128)(2,1)}, u32[]{:S(2)}) copy-start(bf16[256,4096]{1,0:T(8,128)(2,1)} %get-tuple-element.352) | copy-start | bytes 6291460 | tf_op jit(solution)/shard_map/while
  344.3 5.4 copy-start.1
  357.1 2.0 copy-start.2
  366.7 12.3 %copy-start = (f32[512,4096]{1,0:T(8,128)S(1)}, f32[512,4096]{1,0:T(8,128)}, u32[]{:S(2)}) copy-start(f32[512,4096]{1,0:T(8,128)} %fusion.74) | copy-start | bytes 25165828 | tf_op jit(solution)/shard_map/while
  366.7 12.3 %copy-start.5 = (bf16[256,4096]{1,0:T(8,128)(2,1)S(1)}, bf16[256,4096]{1,0:T(8,128)(2,1)}, u32[]{:S(2)}) copy-start(bf16[256,4096]{1,0:T(8,128)(2,1)} %get-tuple-element.352) | copy-start | bytes 6291460 | tf_op jit(solution)/shard_map/while
  379.0 5.4 copy-start.1
  391.8 2.0 copy-start.2
  401.4 12.3 %copy-start = (f32[512,4096]{1,0:T(8,128)S(1)}, f32[512,4096]{1,0:T(8,128)}, u32[]{:S(2)}) copy-start(f32[512,4096]{1,0:T(8,128)} %fusion.74) | copy-start | bytes 25165828 | tf_op jit(solution)/shard_map/while
  401.4 12.3 %copy-start.5 = (bf16[256,4096]{1,0:T(8,128)(2,1)S(1)}, bf16[256,4096]{1,0:T(8,128)(2,1)}, u32[]{:S(2)}) copy-start(bf16[256,4096]{1,0:T(8,128)(2,1)} %get-tuple-element.352) | copy-start | bytes 6291460 | tf_op jit(solution)/shard_map/while
  413.8 5.4 copy-start.1
  426.6 2.0 copy-start.2
  436.1 12.3 %copy-start = (f32[512,4096]{1,0:T(8,128)S(1)}, f32[512,4096]{1,0:T(8,128)}, u32[]{:S(2)}) copy-start(f32[512,4096]{1,0:T(8,128)} %fusion.74) | copy-start | bytes 25165828 | tf_op jit(solution)/shard_map/while
  436.2 12.3 %copy-start.5 = (bf16[256,4096]{1,0:T(8,128)(2,1)S(1)}, bf16[256,4096]{1,0:T(8,128)(2,1)}, u32[]{:S(2)}) copy-start(bf16[256,4096]{1,0:T(8,128)(2,1)} %get-tuple-element.352) | copy-start | bytes 6291460 | tf_op jit(solution)/shard_map/while
  448.5 5.4 copy-start.1
  461.3 2.0 copy-start.2
  470.9 12.3 %copy-start = (f32[512,4096]{1,0:T(8,128)S(1)}, f32[512,4096]{1,0:T(8,128)}, u32[]{:S(2)}) copy-start(f32[512,4096]{1,0:T(8,128)} %fusion.74) | copy-start | bytes 25165828 | tf_op jit(solution)/shard_map/while
  470.9 12.3 %copy-start.5 = (bf16[256,4096]{1,0:T(8,128)(2,1)S(1)}, bf16[256,4096]{1,0:T(8,128)(2,1)}, u32[]{:S(2)}) copy-start(bf16[256,4096]{1,0:T(8,128)(2,1)} %get-tuple-element.352) | copy-start | bytes 6291460 | tf_op jit(solution)/shard_map/while
  483.2 5.4 copy-start.1
  496.0 2.0 copy-start.2
  505.6 12.3 %copy-start = (f32[512,4096]{1,0:T(8,128)S(1)}, f32[512,4096]{1,0:T(8,128)}, u32[]{:S(2)}) copy-start(f32[512,4096]{1,0:T(8,128)} %fusion.74) | copy-start | bytes 25165828 | tf_op jit(solution)/shard_map/while
  505.6 12.3 %copy-start.5 = (bf16[256,4096]{1,0:T(8,128)(2,1)S(1)}, bf16[256,4096]{1,0:T(8,128)(2,1)}, u32[]{:S(2)}) copy-start(bf16[256,4096]{1,0:T(8,128)(2,1)} %get-tuple-element.352) | copy-start | bytes 6291460 | tf_op jit(solution)/shard_map/while
  517.9 5.4 copy-start.1
  540.3 12.3 %copy-start = (f32[512,4096]{1,0:T(8,128)S(1)}, f32[512,4096]{1,0:T(8,128)}, u32[]{:S(2)}) copy-start(f32[512,4096]{1,0:T(8,128)} %fusion.74) | copy-start | bytes 25165828 | tf_op jit(solution)/shard_map/while
  540.3 12.3 %copy-start.5 = (bf16[256,4096]{1,0:T(8,128)(2,1)S(1)}, bf16[256,4096]{1,0:T(8,128)(2,1)}, u32[]{:S(2)}) copy-start(bf16[256,4096]{1,0:T(8,128)(2,1)} %get-tuple-element.352) | copy-start | bytes 6291460 | tf_op jit(solution)/shard_map/while
  552.6 5.4 copy-start.1
  575.0 12.3 %copy-start = (f32[512,4096]{1,0:T(8,128)S(1)}, f32[512,4096]{1,0:T(8,128)}, u32[]{:S(2)}) copy-start(f32[512,4096]{1,0:T(8,128)} %fusion.74) | copy-start | bytes 25165828 | tf_op jit(solution)/shard_map/while
  575.0 12.3 %copy-start.5 = (bf16[256,4096]{1,0:T(8,128)(2,1)S(1)}, bf16[256,4096]{1,0:T(8,128)(2,1)}, u32[]{:S(2)}) copy-start(bf16[256,4096]{1,0:T(8,128)(2,1)} %get-tuple-element.352) | copy-start | bytes 6291460 | tf_op jit(solution)/shard_map/while
  587.4 5.4 copy-start.1
  609.7 12.3 %copy-start = (f32[512,4096]{1,0:T(8,128)S(1)}, f32[512,4096]{1,0:T(8,128)}, u32[]{:S(2)}) copy-start(f32[512,4096]{1,0:T(8,128)} %fusion.74) | copy-start | bytes 25165828 | tf_op jit(solution)/shard_map/while
  609.8 12.3 %copy-start.5 = (bf16[256,4096]{1,0:T(8,128)(2,1)S(1)}, bf16[256,4096]{1,0:T(8,128)(2,1)}, u32[]{:S(2)}) copy-start(bf16[256,4096]{1,0:T(8,128)(2,1)} %get-tuple-element.352) | copy-start | bytes 6291460 | tf_op jit(solution)/shard_map/while
  622.1 5.4 copy-start.1
  644.5 12.3 %copy-start = (f32[512,4096]{1,0:T(8,128)S(1)}, f32[512,4096]{1,0:T(8,128)}, u32[]{:S(2)}) copy-start(f32[512,4096]{1,0:T(8,128)} %fusion.74) | copy-start | bytes 25165828 | tf_op jit(solution)/shard_map/while
  644.5 12.3 %copy-start.5 = (bf16[256,4096]{1,0:T(8,128)(2,1)S(1)}, bf16[256,4096]{1,0:T(8,128)(2,1)}, u32[]{:S(2)}) copy-start(bf16[256,4096]{1,0:T(8,128)(2,1)} %get-tuple-element.352) | copy-start | bytes 6291460 | tf_op jit(solution)/shard_map/while
  656.8 5.4 copy-start.1
  679.2 12.3 %copy-start = (f32[512,4096]{1,0:T(8,128)S(1)}, f32[512,4096]{1,0:T(8,128)}, u32[]{:S(2)}) copy-start(f32[512,4096]{1,0:T(8,128)} %fusion.74) | copy-start | bytes 25165828 | tf_op jit(solution)/shard_map/while
  679.2 12.3 %copy-start.5 = (bf16[256,4096]{1,0:T(8,128)(2,1)S(1)}, bf16[256,4096]{1,0:T(8,128)(2,1)}, u32[]{:S(2)}) copy-start(bf16[256,4096]{1,0:T(8,128)(2,1)} %get-tuple-element.352) | copy-start | bytes 6291460 | tf_op jit(solution)/shard_map/while
  691.5 5.4 copy-start.1
  713.9 12.3 %copy-start = (f32[512,4096]{1,0:T(8,128)S(1)}, f32[512,4096]{1,0:T(8,128)}, u32[]{:S(2)}) copy-start(f32[512,4096]{1,0:T(8,128)} %fusion.74) | copy-start | bytes 25165828 | tf_op jit(solution)/shard_map/while
  713.9 12.3 %copy-start.5 = (bf16[256,4096]{1,0:T(8,128)(2,1)S(1)}, bf16[256,4096]{1,0:T(8,128)(2,1)}, u32[]{:S(2)}) copy-start(bf16[256,4096]{1,0:T(8,128)(2,1)} %get-tuple-element.352) | copy-start | bytes 6291460 | tf_op jit(solution)/shard_map/while
  726.2 5.4 copy-start.1
  748.6 12.3 %copy-start = (f32[512,4096]{1,0:T(8,128)S(1)}, f32[512,4096]{1,0:T(8,128)}, u32[]{:S(2)}) copy-start(f32[512,4096]{1,0:T(8,128)} %fusion.74) | copy-start | bytes 25165828 | tf_op jit(solution)/shard_map/while
  748.6 12.3 %copy-start.5 = (bf16[256,4096]{1,0:T(8,128)(2,1)S(1)}, bf16[256,4096]{1,0:T(8,128)(2,1)}, u32[]{:S(2)}) copy-start(bf16[256,4096]{1,0:T(8,128)(2,1)} %get-tuple-element.352) | copy-start | bytes 6291460 | tf_op jit(solution)/shard_map/while
  761.0 5.4 copy-start.1
  783.3 12.3 %copy-start = (f32[512,4096]{1,0:T(8,128)S(1)}, f32[512,4096]{1,0:T(8,128)}, u32[]{:S(2)}) copy-start(f32[512,4096]{1,0:T(8,128)} %fusion.74) | copy-start | bytes 25165828 | tf_op jit(solution)/shard_map/while
  783.4 12.3 %copy-start.5 = (bf16[256,4096]{1,0:T(8,128)(2,1)S(1)}, bf16[256,4096]{1,0:T(8,128)(2,1)}, u32[]{:S(2)}) copy-start(bf16[256,4096]{1,0:T(8,128)(2,1)} %get-tuple-element.352) | copy-start | bytes 6291460 | tf_op jit(solution)/shard_map/while
  795.7 5.4 copy-start.1
  818.1 12.3 %copy-start = (f32[512,4096]{1,0:T(8,128)S(1)}, f32[512,4096]{1,0:T(8,128)}, u32[]{:S(2)}) copy-start(f32[512,4096]{1,0:T(8,128)} %fusion.74) | copy-start | bytes 25165828 | tf_op jit(solution)/shard_map/while
  818.1 12.3 %copy-start.5 = (bf16[256,4096]{1,0:T(8,128)(2,1)S(1)}, bf16[256,4096]{1,0:T(8,128)(2,1)}, u32[]{:S(2)}) copy-start(bf16[256,4096]{1,0:T(8,128)(2,1)} %get-tuple-element.352) | copy-start | bytes 6291460 | tf_op jit(solution)/shard_map/while
  830.4 5.4 copy-start.1
  873.1 108.8 %reduce-scatter.3.cloned.1.call-start = ((), (), s32[]{:S(2)}) async-start(), calls=%async_computation.8 | async-start | bytes 5242880 | tf_op jit(solution)/shard_map/reduce_scatter | solution.py:82
  886.5 95.5 %copy-start.3 = (bf16[128,2048]{1,0:T(8,128)(2,1)S(1)}, bf16[128,2048]{1,0:T(8,128)(2,1)}, u32[]{:S(2)}) copy-start(bf16[128,2048]{1,0:T(8,128)(2,1)} %param.5) | copy-start | bytes 1572868
  886.5 95.5 %copy-start.4 = (bf16[128,2048]{1,0:T(8,128)(2,1)S(1)}, bf16[128,2048]{1,0:T(8,128)(2,1)}, u32[]{:S(2)}) copy-start(bf16[128,2048]{1,0:T(8,128)(2,1)} %param.4) | copy-start | bytes 1572868
  (10 other events, 19.7 us)
Sparse Core Ops, SparseCore 0:
  9.5 23.9 all-gather.6
  35.1 21.2 all-gather.12
  58.7 82.0 all-gather.8
  142.8 80.5 all-gather.14
  225.4 31.6 all-gather.10
  259.0 33.1 all-gather.16
  873.2 52.6 reduce-scatter.4
  929.2 52.6 reduce-scatter.2
where the time goes:
time: 1040 us; the launch traced here: 1030 us
  matrix products  501 us (48%)
  waiting for transfers between devices  361 us (35%)
  local copies, waits for them, and re-layouts  67.1 us (6%)
  blocking collectives  39.4 us (4%)
  other arithmetic  26.6 us (3%)
  loops' own time  22.2 us (2%)
  between operations  18 us (2%)
    dot_general x32, matrix products, tile_part(): jnp.dot(strip.astype(jnp.float32), off, preferred_element_type=jnp.float3...  315 us
    dot_general x32, matrix products, tile_part(): lax.dot_general(strip, cols, (((0,), (0,)), ((), ())), preferred_element_...  186 us
    all_gather x1, waiting for transfers between devices, on_device(): lax.all_gather(cent_a, 'col', axis=1, tiled=True)  79.1 us
    all_gather x1, waiting for transfers between devices, on_device(): lax.all_gather(cent_b, 'col', axis=1, tiled=True)  78.1 us
    reduce_scatter x1, waiting for transfers between devices, on_device(): lax.psum_scatter(arrange(pull_a), ('dp', 'row'), scatter_dimension=0, til...  56 us
    psum x1, blocking collectives, on_device(): summed = lax.psum(partial_loss, ('dp', 'row', 'col'))  39.4 us
    reduce_scatter x1, waiting for transfers between devices, on_device(): lax.psum_scatter(arrange(pull_b), ('dp', 'row'), scatter_dimension=0, til...  36.9 us
    all_gather x1, waiting for transfers between devices, on_device(): lax.all_gather(cent_b, 'row', axis=1, tiled=True)  35.1 us
  transfers between devices with their start and end apart: 8, of which 8 were waited for; matrix products, arithmetic and copies ran while one was open for 3% of the time, Pallas kernels for 0%

commit v1 on v0

v1 whole, which is shorter than its diff:
```python
import jax
import jax.numpy as jnp
from jax import lax
from jax.sharding import PartitionSpec as P


def on_device(view_a, view_b):
    n_dp = lax.axis_size("dp")
    n_parts = lax.axis_size("row") * lax.axis_size("col")
    dp_index = lax.axis_index("dp")
    n_dev, shard = view_a.shape
    total = n_dev * n_dp
    f_all = shard * n_parts
    coef = 2.0 * total / (25.0 * (total - 1))
    share = shard // n_dp

    own = jnp.stack([view_a, view_b])
    full = lax.all_gather(own, "dp", axis=1, tiled=True).astype(jnp.float32)
    mean = jnp.sum(full, axis=1, keepdims=True) / total
    diff = full - mean
    std = jnp.sqrt(jnp.sum(diff * diff, axis=1, keepdims=True) / (total - 1) + 0.0001)
    cent = diff.astype(jnp.bfloat16)
    cent32 = cent.astype(jnp.float32)
    diag = jnp.sum(cent32 * cent32, axis=1, keepdims=True) / (total - 1)

    piece = lax.dynamic_slice_in_dim(cent, dp_index * share, share, 2)
    gram = lax.dot_general(
        piece, piece, (((2,), (2,)), ((0,), (0,))), preferred_element_type=jnp.float32
    )
    own32 = own.astype(jnp.float32)
    gap = own32[0] - own32[1]
    local = 25.0 * jnp.sum(gap * gap) / (total * f_all)
    per_feature = 25.0 * jnp.maximum(1.0 - std, 0.0) - diag * diag
    local = local + jnp.sum(per_feature) / (f_all * n_dp)
    gram, local = lax.psum((gram, local), ("dp", "row", "col"))
    gram = gram / (total - 1)
    objective = (local + jnp.sum(gram * gram) / f_all) * total / (50.0 * f_all)

    lean = gram - jnp.mean(gram, axis=1, keepdims=True)
    lean = lax.dynamic_slice_in_dim(lean, dp_index * n_dev, n_dev, 1)
    pull = lax.dot_general(
        lean,
        cent32,
        (((2,), (1,)), ((0,), (0,))),
        preferred_element_type=jnp.float32,
        precision=lax.Precision.HIGHEST,
    )
    mine = lax.dynamic_slice_in_dim(cent32, dp_index * n_dev, n_dev, 1)
    pull = pull - diag * (mine - jnp.mean(cent32, axis=1, keepdims=True))
    hinge = jnp.where(std < 1.0, total * (own32 - mean) / (2.0 * std * (total - 1)), 0.0)
    rest = coef * pull - hinge
    return (gap + rest[0], rest[1] - gap, objective)


def solution(mesh):
    in_specs = (P("dp", ("row", "col")), P("dp", ("row", "col")))
    out_specs = (P("dp", ("row", "col")), P("dp", ("row", "col")), P())
    return jax.shard_map(
        on_device, mesh=mesh, in_specs=in_specs, out_specs=out_specs, check_vma=False
    )
```

time: 1040 us -> 239 us (0.23)
  matrix products: 501 us -> 5.1 us
  waiting for transfers between devices: 361 us -> 163 us
  local copies, waits for them, and re-layouts: 67.1 us -> 0.09 us
  loops' own time: 22.2 us -> 0 us
  other arithmetic: 26.6 us -> 12.9 us
    dot_general x64 -> x2, matrix products: 501 us -> 5.1 us  [the longest x1 3.84 us: on_device(): lax.dot_general(lean, cent32, (((2,), (1,)), ((0,), (0,))), preferred_ele...]
    all_gather x6 -> x1, waiting for transfers between devices: 265 us -> 36.3 us  [on_device(): full = lax.all_gather(own, 'dp', axis=1, tiled=True).astype(jnp.float32)]
    psum x0 -> x1, waiting for transfers between devices: none -> 127 us  [on_device(): gram, local = lax.psum((gram, local), ('dp', 'row', 'col'))]
    reduce_scatter x2 -> x0, waiting for transfers between devices: 92.9 us -> none  [the longest x1 56 us: on_device(): lax.psum_scatter(arrange(pull_a), ('dp', 'row'), scatter_dimension=0, til...]
    while x128 -> x0, local copies, waits for them, and re-layouts: 31.5 us -> none
    reshape x4 -> x0, local copies, waits for them, and re-layouts: 26.4 us -> none  [arrange(): term = term.reshape(n_dp, n_dev, n_row, shard).transpose(0, 2, 1, 3)]
    another operation x1 -> x0, loops' own time: 22.2 us -> none  [on_device(): lax.fori_loop(0, row_width // block, one_block, (zeros_pull, zeros_pull,...]
    reduce_sum x9 -> x4, other arithmetic: 17.9 us -> 5.45 us  [the longest x1 2.13 us: on_device(): mean = jnp.sum(full, axis=1, keepdims=True) / total]
  transfers between devices with their start and end apart: 8 -> 2, of which waited for: 8 -> 2; matrix products, arithmetic and copies ran while one was open for 3% -> 0% of each run, Pallas kernels for 0% -> 0%
where the time goes in v1:
time: 239 us; the launch traced here: 238 us
  waiting for transfers between devices  163 us (68%)
  blocking collectives  39.2 us (16%)
  between operations  17.9 us (7%)
  other arithmetic  12.9 us (5%)
  matrix products  5.1 us (2%)
    psum x1, waiting for transfers between devices, on_device(): gram, local = lax.psum((gram, local), ('dp', 'row', 'col'))  127 us
    psum x1, blocking collectives, on_device(): gram, local = lax.psum((gram, local), ('dp', 'row', 'col'))  39.2 us
    all_gather x1, waiting for transfers between devices, on_device(): full = lax.all_gather(own, 'dp', axis=1, tiled=True).astype(jnp.float32)  36.3 us
  transfers between devices with their start and end apart: 2, of which 2 were waited for; matrix products, arithmetic and copies ran while one was open for 0% of the time, Pallas kernels for 0%

profile of v1, /device:TPU:0, one launch (start us, length us, event | category | flops | bytes accessed | tf_op | source)
XLA Modules:
  0.0 238.2 jit_solution(1915178894791776627)
XLA Ops:
  7.2 0.0 all-gather.2.cloned.1.call-start
  7.2 2.4 fusion.13
  9.6 0.0 all-gather.2.cloned.1.call-update
  9.6 0.0 all-reduce.2.cloned.1.call-start
  9.7 36.3 %all-gather.2.cloned.1.call-done = bf16[2,256,2048]{2,1,0:T(8,128)(2,1)} async-done(((bf16[2,128,2048]{2,1,0:T(8,128)(2,1)}), bf16[2,256,2048]{2,1,0:T(8,128)(2,1)}) %all-gather.2.cloned.1.call-update) | async-done | bytes 2097168 | tf_op jit(solution)/shard_map/all_gather | solution.py:18
  46.0 0.0 copy-start.1
  46.0 2.1 convert_reduce_fusion
  48.1 0.1 copy-done.1
  48.2 0.9 multiply_reduce_fusion
  49.1 0.0 copy-start
  49.1 2.6 %convert_element_type.15 = f32[2,256,2048]{2,1,0:T(8,128)} convert(bf16[2,256,2048]{2,1,0:T(8,128)(2,1)S(1)} %get-tuple-element.7) | non-fusion elementwise | flops 1048576 | bytes 6291456 | tf_op jit(solution)/shard_map/convert_element_type | solution.py:23
  51.7 0.0 copy-done
  51.7 0.0 copy-start.2
  51.7 0.0 copy-start.3
  51.7 1.3 fusion.7
  52.9 0.0 all-reduce.2.cloned.1.call-update
  53.0 0.6 subtract_reduce_fusion
  54.3 126.6 %all-reduce.2.cloned.1.call-done = f32[2,256,256]{2,1,0:T(8,128)} async-done(((f32[2,256,256]{2,1,0:T(8,128)}), f32[2,256,256]{2,1,0:T(8,128)}) %all-reduce.2.cloned.1.call-update) | async-done | bytes 524304 | tf_op jit(solution)/shard_map/psum | solution.py:35
  180.9 1.8 multiply_reduce_fusion.2
  182.7 0.0 copy-done.2
  182.7 0.0 copy-done.3
  182.7 3.8 %fusion.4 = f32[2,128,2048]{2,1,0:T(8,128)S(1)} fusion(bf16[2,256,2048]{2,1,0:T(8,128)(2,1)} %copy-done, f32[2,256,2048]{2,1,0:T(8,128)} %convert_element_type.15, s32[]{:T(128)S(6)} %select_n.12, f32[2,2048]{1,0:T(2,128)S(1)} %get-tuple-element.16, f32[2,2048]{1,0:T(2,128)S(1)} %broadcast_multiply_fusion.4, f32[2,2048]{1,0:T(2,128)S(1)} %get-tuple-element.18, ...), kind=kOutput, calls=%fused_computation.8 | convolution fusion | flops 1616445440 | bytes 7678976 | tf_op jit(solution)/shard_map/dot_general | solution.py:41
  186.5 2.4 %fusion.5 = (f32[128,2048]{1,0:T(8,128)}, f32[128,2048]{1,0:T(8,128)}, f32[]{:T(128)}) fusion(f32[2,128,2048]{2,1,0:T(8,128)S(1)} %fusion.4, f32[2,128,2048]{2,1,0:T(8,128)S(1)} %get-tuple-element.12), kind=kLoop, calls=%fused_computation.11 | loop fusion | flops 1310719 | bytes 6291460 | tf_op jit(solution)/shard_map/sub | solution.py:52
  189.7 39.2 %psum.15 = f32[]{:T(128)} all-reduce(f32[]{:T(128)S(6)} %add.45), channel_id=1, replica_groups=mesh['dp'=2,'row'=2,'col'=8] {'dp','row','col'}, use_global_device_ids=true, to_apply=%region_8.0 | all-reduce | flops 1 | bytes 8 | tf_op jit(solution)/shard_map/psum | solution.py:35
  (3 shorter events, 0.0 us)
Async XLA Ops:
  7.2 38.8 %all-gather.2.cloned.1.call-start = ((), (), s32[]{:S(2)}) async-start(), calls=%async_computation | async-start | bytes 3145728 | tf_op jit(solution)/shard_map/all_gather | solution.py:18
  9.6 171.3 %all-reduce.2.cloned.1.call-start = ((), (), s32[]{:S(2)}) async-start(), calls=%async_computation.1 | async-start | bytes 1048576 | tf_op jit(solution)/shard_map/psum | solution.py:35
  46.0 2.2 copy-start.1
  49.1 2.6 %copy-start = (bf16[2,256,2048]{2,1,0:T(8,128)(2,1)}, bf16[2,256,2048]{2,1,0:T(8,128)(2,1)S(1)}, u32[]{:S(2)}) copy-start(bf16[2,256,2048]{2,1,0:T(8,128)(2,1)S(1)} %get-tuple-element.7) | copy-start | bytes 6291460
  51.7 131.0 %copy-start.2 = (bf16[128,2048]{1,0:T(8,128)(2,1)S(1)}, bf16[128,2048]{1,0:T(8,128)(2,1)}, u32[]{:S(2)}) copy-start(bf16[128,2048]{1,0:T(8,128)(2,1)} %param.3) | copy-start | bytes 1572868
  51.7 131.0 %copy-start.3 = (bf16[128,2048]{1,0:T(8,128)(2,1)S(1)}, bf16[128,2048]{1,0:T(8,128)(2,1)}, u32[]{:S(2)}) copy-start(bf16[128,2048]{1,0:T(8,128)(2,1)} %param.2) | copy-start | bytes 1572868
Sparse Core Ops, SparseCore 0:
  10.1 35.8 all-gather.1
  53.1 127.7 all-reduce.1

commit v2 on v1

--- a/solution.py
+++ b/solution.py
@@ -1,10 +1,18 @@
+import functools
+
 import jax
 import jax.numpy as jnp
 from jax import lax
+from jax.experimental import pallas as pl
+from jax.experimental.pallas import tpu as pltpu
 from jax.sharding import PartitionSpec as P
 
-
-def on_device(view_a, view_b):
+LANES = 128
+TILE = 8
+MESH = pl.DeviceIdType.MESH
+
+
+def plain(view_a, view_b):
     n_dp = lax.axis_size("dp")
     n_parts = lax.axis_size("row") * lax.axis_size("col")
     dp_index = lax.axis_index("dp")
@@ -52,6 +60,285 @@
     return (gap + rest[0], rest[1] - gap, objective)
 
 
+def gram_kernel(
+    n_row,
+    n_col,
+    view_a,
+    view_b,
+    grad_a,
+    grad_b,
+    loss_out,
+    other,
+    cent,
+    stats,
+    gram,
+    extra,
+    local,
+    outgoing,
+    incoming,
+    summed,
+    loss_in,
+    view_send,
+    view_recv,
+    part_send,
+    part_recv,
+    sum_send,
+    sum_recv,
+    loss_send,
+    loss_recv,
+):
+    views = (view_a, view_b)
+    n_dev, shard = view_a.shape
+    total = 2 * n_dev
+    n_plane = n_row * n_col
+    f_all = shard * n_plane
+    coef = 2.0 * total / (25.0 * (total - 1))
+    n_chunks = other.shape[0]
+    width = other.shape[3]
+    rows = summed.shape[1]
+    dp = lax.axis_index("dp")
+    me = lax.axis_index("row") * n_col + lax.axis_index("col")
+    partner = {"dp": 1 - dp}
+
+    def place(peer):
+        return {"row": peer // n_col, "col": peer % n_col}
+
+    barrier = pltpu.get_barrier_semaphore()
+    pl.semaphore_signal(barrier, inc=1, device_id=partner, device_id_type=MESH)
+
+    def greet(k, carry):
+        peer = (me + k) % n_plane
+        pl.semaphore_signal(barrier, inc=1, device_id=place(peer), device_id_type=MESH)
+        return carry
+
+    lax.fori_loop(1, n_plane, greet, 0)
+    pl.semaphore_wait(barrier, n_plane)
+
+    def view_copy(v, c):
+        return pltpu.make_async_remote_copy(
+            src_ref=views[v].at[:, pl.ds(pl.multiple_of(c * width, width), width)],
+            dst_ref=other.at[c, v],
+            send_sem=view_send.at[c, v],
+            recv_sem=view_recv.at[c, v],
+            device_id=partner,
+            device_id_type=MESH,
+        )
+
+    def send_views(c, carry):
+        view_copy(0, c).start()
+        view_copy(1, c).start()
+        return carry
+
+    lax.fori_loop(0, n_chunks, send_views, 0)
+    gram[...] = jnp.zeros_like(gram)
+    extra[...] = jnp.zeros_like(extra)
+    local[...] = jnp.zeros_like(local)
+
+    def over(x, y):
+        return jnp.sum(x, axis=0, keepdims=True) + jnp.sum(y, axis=0, keepdims=True)
+
+    def take_chunk(c, carry):
+        cols = pl.ds(pl.multiple_of(c * width, width), width)
+        values = []
+        for v in range(2):
+            view_copy(v, c).wait()
+            mine = views[v][:, cols].astype(jnp.float32)
+            theirs = other[c, v].astype(jnp.float32)
+            values.append((mine, theirs))
+            mean = over(mine, theirs) / total
+            mine = mine - mean
+            theirs = theirs - mean
+            std = jnp.sqrt(over(mine * mine, theirs * theirs) / (total - 1) + 0.0001)
+            cent[v, 0:n_dev, cols] = mine.astype(jnp.bfloat16)
+            cent[v, n_dev:total, cols] = theirs.astype(jnp.bfloat16)
+            mine = cent[v, 0:n_dev, cols].astype(jnp.float32)
+            theirs = cent[v, n_dev:total, cols].astype(jnp.float32)
+            diag = over(mine * mine, theirs * theirs) / (total - 1)
+            column = over(mine, theirs)
+            stats[v, 0:1, cols] = mean
+            stats[v, 1:2, cols] = jnp.where(std < 1.0, total / (2.0 * std * (total - 1)), 0.0)
+            stats[v, 2:3, cols] = diag * coef
+            stats[v, 3:4, cols] = column / total
+            local[...] += (25.0 * jnp.maximum(1.0 - std, 0.0) - diag * diag) / f_all
+            high = column.astype(jnp.bfloat16).astype(jnp.float32)
+            row = lax.broadcasted_iota(jnp.int32, (16, width), 0)
+            parts = jnp.where(row == 0, high, jnp.where(row == 1, column - high, 0.0))
+            both = cent[v, :, cols]
+            dims = (((1,), (1,)), ((), ()))
+            gram[v] += lax.dot_general(
+                cent[v, 0:n_dev, cols], both, dims, preferred_element_type=jnp.float32
+            )
+            extra[v] += lax.dot_general(
+                parts.astype(jnp.bfloat16), both, dims, preferred_element_type=jnp.float32
+            )
+        gap_mine = values[0][0] - values[1][0]
+        gap_theirs = values[0][1] - values[1][1]
+        local[...] += 25.0 * over(gap_mine * gap_mine, gap_theirs * gap_theirs) / (total * f_all)
+        return carry
+
+    lax.fori_loop(0, n_chunks, take_chunk, 0)
+
+    small = [jnp.sum(extra[v], axis=0, keepdims=True) for v in range(2)]
+    local_sum = jnp.broadcast_to(jnp.sum(local[...]).reshape(1, 1), (1, LANES))
+    tail = jnp.concatenate(
+        [small[v][:, h * LANES:(h + 1) * LANES] for v in range(2) for h in range(2)]
+        + [local_sum, jnp.zeros((TILE - 5, LANES), jnp.float32)],
+        axis=0,
+    )
+    per_block = n_dev // rows
+    for r in range(n_plane):
+        v, h, q = r // (2 * per_block), r // per_block % 2, r % per_block
+        outgoing[r, 0:rows, :] = gram[v, q * rows:(q + 1) * rows, h * LANES:(h + 1) * LANES]
+        outgoing[r, rows:rows + TILE, :] = tail
+
+    def part_copy(peer, slot):
+        return pltpu.make_async_remote_copy(
+            src_ref=outgoing.at[peer],
+            dst_ref=incoming.at[slot],
+            send_sem=part_send.at[peer],
+            recv_sem=part_recv.at[slot],
+            device_id=place(peer),
+            device_id_type=MESH,
+        )
+
+    def start_part(k, carry):
+        part_copy((me + k) % n_plane, me).start()
+        return carry
+
+    def end_part(k, carry):
+        peer = (me + k) % n_plane
+        part_copy(peer, peer).wait()
+        return carry
+
+    lax.fori_loop(1, n_plane, start_part, 0)
+    incoming[me] = outgoing[me]
+    lax.fori_loop(1, n_plane, end_part, 0)
+    piece = incoming[0]
+    for r in range(1, n_plane):
+        piece = piece + incoming[r]
+    summed[me] = piece[0:rows, :]
+    tail = piece[rows:rows + TILE, :]
+
+    def sum_copy(peer, slot):
+        return pltpu.make_async_remote_copy(
+            src_ref=summed.at[slot],
+            dst_ref=summed.at[slot],
+            send_sem=sum_send.at[peer],
+            recv_sem=sum_recv.at[slot],
+            device_id=place(peer),
+            device_id_type=MESH,
+        )
+
+    def start_sum(k, carry):
+        sum_copy((me + k) % n_plane, me).start()
+        return carry
+
+    def end_sum(k, carry):
+        peer = (me + k) % n_plane
+        sum_copy(peer, me).wait_send()
+        sum_copy(peer, peer).wait_recv()
+        return carry
+
+    lax.fori_loop(1, n_plane, start_sum, 0)
+    lax.fori_loop(1, n_plane, end_sum, 0)
+
+    square = jnp.zeros((rows, LANES), jnp.float32)
+    for r in range(n_plane):
+        square = square + summed[r] * summed[r]
+    scale = 1.0 / (float(total - 1) * float(total - 1) * f_all)
+    square = jnp.broadcast_to(jnp.sum(square).reshape(1, 1), (TILE, LANES)) * scale
+    share = square + 0.5 * jnp.broadcast_to(tail[4:5, :], (TILE, LANES))
+    loss_in[0] = share
+    loss_copy = pltpu.make_async_remote_copy(
+        src_ref=loss_in.at[0],
+        dst_ref=loss_in.at[1],
+        send_sem=loss_send,
+        recv_sem=loss_recv,
+        device_id=partner,
+        device_id_type=MESH,
+    )
+    loss_copy.start()
+
+    factors = []
+    for v in range(2):
+        halves = []
+        for h in range(2):
+            first = (v * 2 + h) * per_block
+            block = jnp.concatenate([summed[first + q] for q in range(per_block)], axis=0)
+            halves.append(block - tail[v * 2 + h:v * 2 + h + 1, :] / total)
+        factor = jnp.concatenate(halves, axis=1) * (coef / (total - 1))
+        one = factor.astype(jnp.bfloat16)
+        rest = factor - one.astype(jnp.float32)
+        two = rest.astype(jnp.bfloat16)
+        three = (rest - two.astype(jnp.float32)).astype(jnp.bfloat16)
+        factors.append(jnp.concatenate([one, two, three], axis=0))
+
+    def give_chunk(c, carry):
+        cols = pl.ds(pl.multiple_of(c * width, width), width)
+        results = []
+        mine = [views[v][:, cols].astype(jnp.float32) for v in range(2)]
+        gap = mine[0] - mine[1]
+        for v in range(2):
+            pull = jnp.dot(factors[v], cent[v, :, cols], preferred_element_type=jnp.float32)
+            pull = pull[0:n_dev] + pull[n_dev:total] + pull[total:total + n_dev]
+            kept = cent[v, 0:n_dev, cols].astype(jnp.float32)
+            pull = pull - stats[v, 2:3, cols] * (kept - stats[v, 3:4, cols])
+            results.append(pull - stats[v, 1:2, cols] * (mine[v] - stats[v, 0:1, cols]))
+        grad_a[:, cols] = gap + results[0]
+        grad_b[:, cols] = results[1] - gap
+        return carry
+
+    lax.fori_loop(0, n_chunks, give_chunk, 0)
+    loss_copy.wait()
+    loss_out[...] = (loss_in[0] + loss_in[1]) * (total / (50.0 * f_all))
+
+
+def on_device(view_a, view_b):
+    n_row = lax.axis_size("row")
+    n_col = lax.axis_size("col")
+    n_plane = n_row * n_col
+    n_dev, shard = view_a.shape
+    rows = 4 * n_dev // n_plane
+    fits = n_dev == LANES and rows % TILE == 0 and n_dev % rows == 0
+    if lax.axis_size("dp") != 2 or not fits or shard % LANES:
+        return plain(view_a, view_b)
+    total = 2 * n_dev
+    n_chunks = 4 if shard % (4 * LANES) == 0 else 1
+    width = shard // n_chunks
+    space = pl.BlockSpec(memory_space=pltpu.VMEM)
+    grad = jax.ShapeDtypeStruct((n_dev, shard), jnp.float32)
+    grad_a, grad_b, loss = pl.pallas_call(
+        functools.partial(gram_kernel, n_row, n_col),
+        out_shape=(grad, grad, jax.ShapeDtypeStruct((TILE, LANES), jnp.float32)),
+        in_specs=[space] * 2,
+        out_specs=(space,) * 3,
+        scratch_shapes=[
+            pltpu.VMEM((n_chunks, 2, n_dev, width), jnp.bfloat16),
+            pltpu.VMEM((2, total, shard), jnp.bfloat16),
+            pltpu.VMEM((2, TILE, shard), jnp.float32),
+            pltpu.VMEM((2, n_dev, total), jnp.float32),
+            pltpu.VMEM((2, 16, total), jnp.float32),
+            pltpu.VMEM((1, width), jnp.float32),
+            pltpu.VMEM((n_plane, rows + TILE, LANES), jnp.float32),
+            pltpu.VMEM((n_plane, rows + TILE, LANES), jnp.float32),
+            pltpu.VMEM((n_plane, rows, LANES), jnp.float32),
+            pltpu.VMEM((2, TILE, LANES), jnp.float32),
+            pltpu.SemaphoreType.DMA((n_chunks, 2)),
+            pltpu.SemaphoreType.DMA((n_chunks, 2)),
+            pltpu.SemaphoreType.DMA((n_plane,)),
+            pltpu.SemaphoreType.DMA((n_plane,)),
+            pltpu.SemaphoreType.DMA((n_plane,)),
+            pltpu.SemaphoreType.DMA((n_plane,)),
+            pltpu.SemaphoreType.DMA,
+            pltpu.SemaphoreType.DMA,
+        ],
+        compiler_params=pltpu.CompilerParams(
+            collective_id=0, has_side_effects=True, vmem_limit_bytes=32 * 1024 * 1024
+        ),
+    )(view_a, view_b)
+    return (grad_a, grad_b, loss[0, 0])
+
+
 def solution(mesh):
     in_specs = (P("dp", ("row", "col")), P("dp", ("row", "col")))
     out_specs = (P("dp", ("row", "col")), P("dp", ("row", "col")), P())

time: 239 us -> 54.8 us (0.23)
  waiting for transfers between devices: 163 us -> 0 us
  Pallas kernels: 0 us -> 49.4 us
  blocking collectives: 39.2 us -> 0 us
  between operations: 17.9 us -> 0.65 us
  other arithmetic: 12.9 us -> 0 us
  matrix products: 5.1 us -> 0 us
  local copies, waits for them, and re-layouts: 0.09 us -> 4.53 us
    psum x1 -> x0, waiting for transfers between devices: 127 us -> none  [on_device(): gram, local = lax.psum((gram, local), ('dp', 'row', 'col'))]
    pallas_call x0 -> x1, Pallas kernels: none -> 49.4 us  [on_device(): pl.pallas_call(functools.partial(gram_kernel, n_row, n_col), out_shape=(g...]
    psum x1 -> x0, blocking collectives: 39.2 us -> none  [on_device(): gram, local = lax.psum((gram, local), ('dp', 'row', 'col'))]
    all_gather x1 -> x0, waiting for transfers between devices: 36.3 us -> none  [on_device(): full = lax.all_gather(own, 'dp', axis=1, tiled=True).astype(jnp.float32)]
    reduce_sum x4 -> x0, other arithmetic: 5.45 us -> none  [the longest x1 2.13 us: on_device(): mean = jnp.sum(full, axis=1, keepdims=True) / total]
    dot_general x2 -> x0, matrix products: 5.1 us -> none  [the longest x1 3.84 us: on_device(): lax.dot_general(lean, cent32, (((2,), (1,)), ((0,), (0,))), preferred_ele...]
    convert_element_type x2 -> x0, other arithmetic: 4.93 us -> none  [the longest x1 2.56 us: on_device(): cent32 = cent.astype(jnp.float32)]
    unnamed x8 -> x6, local copies, waits for them, and re-layouts: 0.09 us -> 4.01 us
  transfers between devices with their start and end apart: 2 -> 0, of which waited for: 2 -> 0; matrix products, arithmetic and copies ran while one was open for 0% -> 0% of each run, Pallas kernels for 0% -> 0%
where the time goes in v2:
time: 54.8 us; the launch traced here: 54.5 us
  Pallas kernels  49.4 us (90%)
  local copies, waits for them, and re-layouts  4.53 us (8%)
  between operations  0.65 us (1%)
    pallas_call x1, Pallas kernels, on_device(): pl.pallas_call(functools.partial(gram_kernel, n_row, n_col), out_shape=(g...  49.4 us
    unnamed x6, local copies, waits for them, and re-layouts  4.01 us

profile of v2, /device:TPU:0, one launch (start us, length us, event | category | flops | bytes accessed | tf_op | source)
XLA Modules:
  0.0 54.5 jit_solution(13090429848447349865)
XLA Ops:
  0.6 0.0 copy-start
  0.6 1.0 %copy-done = bf16[128,2048]{1,0:T(8,128)(2,1)S(1)} copy-done((bf16[128,2048]{1,0:T(8,128)(2,1)S(1)}, bf16[128,2048]{1,0:T(8,128)(2,1)}, u32[]{:S(2)}) %copy-start) | copy-done | bytes 524312
  1.7 0.0 copy-start.1
  1.7 1.0 %copy-done.1 = bf16[128,2048]{1,0:T(8,128)(2,1)S(1)} copy-done((bf16[128,2048]{1,0:T(8,128)(2,1)S(1)}, bf16[128,2048]{1,0:T(8,128)(2,1)}, u32[]{:S(2)}) %copy-start.1) | copy-done | bytes 524312
  2.7 49.4 %shard_map.49 = (f32[128,2048]{1,0:T(8,128)S(1)}, f32[128,2048]{1,0:T(8,128)S(1)}, f32[8,128]{1,0:T(8,128)S(1)}) custom-call(bf16[128,2048]{1,0:T(8,128)(2,1)S(1)} %copy-done, bf16[128,2048]{1,0:T(8,128)(2,1)S(1)} %copy-done.1), custom_call_target="tpu_custom_call" | custom-call | tf_op jit(solution)/shard_map/pallas_call | solution.py:310
  52.1 0.5 slice.3
  52.6 1.0 %copy.7 = f32[128,2048]{1,0:T(8,128)} copy(f32[128,2048]{1,0:T(8,128)S(1)} %get-tuple-element.12) | data formatting | bytes 2097152
  53.6 1.0 %copy.8 = f32[128,2048]{1,0:T(8,128)} copy(f32[128,2048]{1,0:T(8,128)S(1)} %get-tuple-element.13) | data formatting | bytes 2097152
Async XLA Ops:
  0.6 1.0 %copy-start = (bf16[128,2048]{1,0:T(8,128)(2,1)S(1)}, bf16[128,2048]{1,0:T(8,128)(2,1)}, u32[]{:S(2)}) copy-start(bf16[128,2048]{1,0:T(8,128)(2,1)} %view_a.1) | copy-start | bytes 1572868
  1.7 1.0 %copy-start.1 = (bf16[128,2048]{1,0:T(8,128)(2,1)S(1)}, bf16[128,2048]{1,0:T(8,128)(2,1)}, u32[]{:S(2)}) copy-start(bf16[128,2048]{1,0:T(8,128)(2,1)} %view_b.1) | copy-start | bytes 1572868

commit v3 on v1

--- a/solution.py
+++ b/solution.py
@@ -1,10 +1,18 @@
+import functools
+
 import jax
 import jax.numpy as jnp
 from jax import lax
+from jax.experimental import pallas as pl
+from jax.experimental.pallas import tpu as pltpu
 from jax.sharding import PartitionSpec as P
 
-
-def on_device(view_a, view_b):
+LANES = 128
+TILE = 8
+MESH = pl.DeviceIdType.MESH
+
+
+def plain(view_a, view_b):
     n_dp = lax.axis_size("dp")
     n_parts = lax.axis_size("row") * lax.axis_size("col")
     dp_index = lax.axis_index("dp")
@@ -52,6 +60,371 @@
     return (gap + rest[0], rest[1] - gap, objective)
 
 
+def gram_kernel(
+    n_row,
+    n_col,
+    view_a,
+    view_b,
+    grad_a,
+    grad_b,
+    loss_out,
+    mine,
+    other,
+    cent,
+    stats,
+    sums,
+    gram_own,
+    gram_cross,
+    extra,
+    local,
+    out_own,
+    in_own,
+    all_own,
+    out_cross,
+    in_cross,
+    all_cross,
+    pair,
+    load_sem,
+    view_send,
+    view_recv,
+    sums_sem,
+    pair_sem,
+    own_send,
+    own_recv,
+    own_all_send,
+    own_all_recv,
+    cross_send,
+    cross_recv,
+    cross_all_send,
+    cross_all_recv,
+):
+    views = (view_a, view_b)
+    grads = (grad_a, grad_b)
+    n_dev, shard = view_a.shape
+    total = 2 * n_dev
+    n_plane = n_row * n_col
+    f_all = shard * n_plane
+    coef = 2.0 * total / (25.0 * (total - 1))
+    n_chunks = other.shape[0]
+    half = n_chunks // 2
+    width = other.shape[3]
+    rows = all_own.shape[1]
+    dp = lax.axis_index("dp")
+    me = lax.axis_index("row") * n_col + lax.axis_index("col")
+    partner = {"dp": 1 - dp}
+
+    def columns(c):
+        return pl.ds(pl.multiple_of(c * width, width), width)
+
+    def load(v, c):
+        return pltpu.make_async_copy(
+            views[v].at[:, columns(c)], mine.at[v, :, columns(c)], load_sem.at[c, v]
+        )
+
+    for c in range(n_chunks):
+        load(0, c).start()
+        load(1, c).start()
+
+    def place(peer):
+        return {"row": peer // n_col, "col": peer % n_col}
+
+    barrier = pltpu.get_barrier_semaphore()
+    pl.semaphore_signal(barrier, inc=1, device_id=partner, device_id_type=MESH)
+
+    def greet(k, carry):
+        peer = (me + k) % n_plane
+        pl.semaphore_signal(barrier, inc=1, device_id=place(peer), device_id_type=MESH)
+        return carry
+
+    lax.fori_loop(1, n_plane, greet, 0)
+    pl.semaphore_wait(barrier, n_plane)
+
+    def to_partner(source, target, send_sem, recv_sem):
+        return pltpu.make_async_remote_copy(
+            src_ref=source,
+            dst_ref=target,
+            send_sem=send_sem,
+            recv_sem=recv_sem,
+            device_id=partner,
+            device_id_type=MESH,
+        )
+
+    def view_copy(v, c):
+        return to_partner(
+            views[v].at[:, columns(c)], other.at[c, v], view_send.at[c, v], view_recv.at[c, v]
+        )
+
+    def send_views(k, carry):
+        c = (half * (1 - dp) + k) % n_chunks
+        view_copy(0, c).start()
+        view_copy(1, c).start()
+        return carry
+
+    lax.fori_loop(0, 1, send_views, 0)
+
+    def add_rows(x):
+        return jnp.sum(x, axis=0, keepdims=True)
+
+    def own_sums(c, carry):
+        for v in range(2):
+            load(v, c).wait()
+            sums[0, v:v + 1, columns(c)] = add_rows(mine[v, :, columns(c)].astype(jnp.float32))
+        return carry
+
+    lax.fori_loop(0, n_chunks, own_sums, 0)
+    sums_copy = to_partner(sums.at[0], sums.at[1], sums_sem.at[0], sums_sem.at[1])
+    sums_copy.start()
+    lax.fori_loop(1, n_chunks, send_views, 0)
+    gram_own[...] = jnp.zeros_like(gram_own)
+    gram_cross[...] = jnp.zeros_like(gram_cross)
+    extra[...] = jnp.zeros_like(extra)
+    local[...] = jnp.zeros_like(local)
+    sums_copy.wait()
+    dims = (((1,), (1,)), ((), ()))
+
+    def center_own(c, carry):
+        cols = columns(c)
+        for v in range(2):
+            mean = (sums[0, v:v + 1, cols] + sums[1, v:v + 1, cols]) / total
+            diff = mine[v, :, cols].astype(jnp.float32) - mean
+            kept = diff.astype(jnp.bfloat16)
+            cent[v, dp, :, cols] = kept
+            back = kept.astype(jnp.float32)
+            stats[v, 0:1, cols] = mean
+            stats[v, 4:5, cols] = add_rows(diff * diff)
+            stats[v, 5:6, cols] = add_rows(back * back)
+            stats[v, 6:7, cols] = add_rows(back)
+            gram_own[v] += lax.dot_general(kept, kept, dims, preferred_element_type=jnp.float32)
+        return carry
+
+    lax.fori_loop(0, n_chunks, center_own, 0)
+
+    def exchange(source, target, send_sem, recv_sem, scatter):
+        def copy(peer, slot):
+            return pltpu.make_async_remote_copy(
+                src_ref=source.at[peer if scatter else slot],
+                dst_ref=target.at[slot],
+                send_sem=send_sem.at[peer],
+                recv_sem=recv_sem.at[slot],
+                device_id=place(peer),
+                device_id_type=MESH,
+            )
+
+        def start_one(k, carry):
+            copy((me + k) % n_plane, me).start()
+            return carry
+
+        def end_one(k, carry):
+            peer = (me + k) % n_plane
+            copy(peer, me).wait_send()
+            copy(peer, peer).wait_recv()
+            return carry
+
+        def start():
+            lax.fori_loop(1, n_plane, start_one, 0)
+
+        def end():
+            lax.fori_loop(1, n_plane, end_one, 0)
+
+        return start, end
+
+    def added(ref):
+        piece = ref[0]
+        for r in range(1, n_plane):
+            piece = piece + ref[r]
+        return piece
+
+    start_own, end_own = exchange(out_own, in_own, own_send, own_recv, True)
+    start_own_all, end_own_all = exchange(all_own, all_own, own_all_send, own_all_recv, False)
+    start_cross, end_cross = exchange(out_cross, in_cross, cross_send, cross_recv, True)
+    start_cross_all, end_cross_all = exchange(
+        all_cross, all_cross, cross_all_send, cross_all_recv, False
+    )
+    per_block = n_dev // rows
+    for r in range(n_plane):
+        first = r % per_block * rows
+        out_own[r] = gram_own[r // per_block, first:first + rows, :]
+    start_own()
+    in_own[me] = out_own[me]
+
+    def take_chunk(k, multiply):
+        c = (half * dp + k) % n_chunks
+        cols = columns(c)
+        both = [mine[v, :, cols].astype(jnp.float32) for v in range(2)]
+        gap = both[0] - both[1]
+        for v in range(2):
+            view_copy(v, c).wait_recv()
+            mean = stats[v, 0:1, cols]
+            diff = other[c, v].astype(jnp.float32) - mean
+            kept = diff.astype(jnp.bfloat16)
+            cent[v, 1 - dp, :, cols] = kept
+            back = kept.astype(jnp.float32)
+            std = jnp.sqrt((stats[v, 4:5, cols] + add_rows(diff * diff)) / (total - 1) + 0.0001)
+            diag = (stats[v, 5:6, cols] + add_rows(back * back)) / (total - 1)
+            column = stats[v, 6:7, cols] + add_rows(back)
+            slope = jnp.where(std < 1.0, total / (2.0 * std * (total - 1)), 0.0)
+            own = cent[v, dp, :, cols].astype(jnp.float32)
+            rest = slope * (both[v] - mean) + (coef * diag) * (own - column / total)
+            grads[v][:, cols] = (gap if v == 0 else -gap) - rest
+            if multiply:
+                local[...] += (25.0 * jnp.maximum(1.0 - std, 0.0) - diag * diag) / f_all
+                high = column.astype(jnp.bfloat16).astype(jnp.float32)
+                row = lax.broadcasted_iota(jnp.int32, (16, width), 0)
+                parts = jnp.where(row == 0, high, jnp.where(row == 1, column - high, 0.0))
+                gram_cross[v] += lax.dot_general(
+                    cent[v, 0, :, cols],
+                    cent[v, 1, :, cols],
+                    dims,
+                    preferred_element_type=jnp.float32,
+                )
+                for h in range(2):
+                    extra[v, h] += lax.dot_general(
+                        parts.astype(jnp.bfloat16),
+                        cent[v, h, :, cols],
+                        dims,
+                        preferred_element_type=jnp.float32,
+                    )
+        if multiply:
+            gap_other = other[c, 0].astype(jnp.float32) - other[c, 1].astype(jnp.float32)
+            squares = add_rows(gap * gap) + add_rows(gap_other * gap_other)
+            local[...] += 25.0 * squares / (total * f_all)
+
+    take_chunk(0, True)
+    end_own()
+    all_own[me] = added(in_own)
+    start_own_all()
+    for k in range(1, half):
+        take_chunk(k, True)
+
+    local_sum = jnp.broadcast_to(jnp.sum(local[...]).reshape(1, 1), (1, LANES))
+    tail = jnp.concatenate(
+        [add_rows(extra[v, h]) for v in range(2) for h in range(2)]
+        + [local_sum, jnp.zeros((TILE - 5, LANES), jnp.float32)],
+        axis=0,
+    )
+    for r in range(n_plane):
+        first = r % per_block * rows
+        out_cross[r, 0:rows, :] = gram_cross[r // per_block, first:first + rows, :]
+        out_cross[r, rows:rows + TILE, :] = tail
+    start_cross()
+    in_cross[me] = out_cross[me]
+    end_own_all()
+
+    def squared(ref):
+        square = jnp.zeros((rows, LANES), jnp.float32)
+        for r in range(n_plane):
+            square = square + ref[r] * ref[r]
+        return jnp.broadcast_to(jnp.sum(square).reshape(1, 1), (1, LANES))
+
+    own_square = squared(all_own)
+    end_cross()
+    piece = added(in_cross)
+    pair[0] = piece
+    pair[0, rows + 5:rows + 6, :] = own_square
+    pair_copy = to_partner(pair.at[0], pair.at[1], pair_sem.at[0], pair_sem.at[1])
+    pair_copy.start()
+    for k in range(half, n_chunks - 1):
+        take_chunk(k, False)
+    pair_copy.wait()
+    piece = pair[0] + pair[1]
+    all_cross[me] = piece[0:rows, :]
+    start_cross_all()
+    tail = piece[rows:rows + TILE, :]
+    end_cross_all()
+
+    first_half = jnp.full((n_dev, LANES), dp, jnp.int32) == 0
+    factors = []
+    for v in range(2):
+        span = range(v * per_block, (v + 1) * per_block)
+        own = jnp.concatenate([all_own[r] for r in span], axis=0)
+        cross = jnp.concatenate([all_cross[r] for r in span], axis=0)
+        left = jnp.where(first_half, own, cross.T) - tail[2 * v:2 * v + 1, :] / total
+        right = jnp.where(first_half, cross, own) - tail[2 * v + 1:2 * v + 2, :] / total
+        factor = jnp.concatenate([left, right], axis=1) * (coef / (total - 1))
+        one = factor.astype(jnp.bfloat16)
+        rest = factor - one.astype(jnp.float32)
+        two = rest.astype(jnp.bfloat16)
+        three = (rest - two.astype(jnp.float32)).astype(jnp.bfloat16)
+        factors.append(jnp.concatenate([one, two, three], axis=0))
+
+    def give_chunk(k, carry):
+        cols = columns((half * dp + k) % n_chunks)
+        for v in range(2):
+            right = cent[v, :, :, cols].reshape(total, width)
+            pull = jnp.dot(factors[v], right, preferred_element_type=jnp.float32)
+            grads[v][:, cols] += pull[0:n_dev] + pull[n_dev:total] + pull[total:total + n_dev]
+        return carry
+
+    lax.fori_loop(0, n_chunks - 1, give_chunk, 0)
+    square = tail[5:6, :] + 2.0 * squared(all_cross)
+    loss = tail[4:5, :] + square / (float(total - 1) * float(total - 1) * f_all)
+    loss_out[...] = jnp.broadcast_to(loss * (total / (50.0 * f_all)), (TILE, LANES))
+    take_chunk(n_chunks - 1, False)
+    give_chunk(n_chunks - 1, 0)
+
+    def end_views(c, carry):
+        view_copy(0, c).wait_send()
+        view_copy(1, c).wait_send()
+        return carry
+
+    lax.fori_loop(0, n_chunks, end_views, 0)
+
+
+def on_device(view_a, view_b):
+    n_row = lax.axis_size("row")
+    n_col = lax.axis_size("col")
+    n_plane = n_row * n_col
+    n_dev, shard = view_a.shape
+    total = 2 * n_dev
+    rows = total // n_plane
+    n_chunks = 4
+    width = shard // n_chunks
+    fits = n_dev == LANES and rows > 0 and rows % TILE == 0 and n_dev % rows == 0
+    if lax.axis_size("dp") != 2 or not fits or shard % (n_chunks * LANES):
+        return plain(view_a, view_b)
+    space = pl.BlockSpec(memory_space=pltpu.VMEM)
+    grad = jax.ShapeDtypeStruct((n_dev, shard), jnp.float32)
+    own_part = pltpu.VMEM((n_plane, rows, LANES), jnp.float32)
+    cross_part = pltpu.VMEM((n_plane, rows + TILE, LANES), jnp.float32)
+    plane_sems = pltpu.SemaphoreType.DMA((n_plane,))
+    chunk_sems = pltpu.SemaphoreType.DMA((n_chunks, 2))
+    pair_sems = pltpu.SemaphoreType.DMA((2,))
+    grad_a, grad_b, loss = pl.pallas_call(
+        functools.partial(gram_kernel, n_row, n_col),
+        out_shape=(grad, grad, jax.ShapeDtypeStruct((TILE, LANES), jnp.float32)),
+        in_specs=[pl.BlockSpec(memory_space=pl.ANY)] * 2,
+        out_specs=(space,) * 3,
+        scratch_shapes=[
+            pltpu.VMEM((2, n_dev, shard), jnp.bfloat16),
+            pltpu.VMEM((n_chunks, 2, n_dev, width), jnp.bfloat16),
+            pltpu.VMEM((2, 2, n_dev, shard), jnp.bfloat16),
+            pltpu.VMEM((2, TILE, shard), jnp.float32),
+            pltpu.VMEM((2, 2, shard), jnp.float32),
+            pltpu.VMEM((2, n_dev, LANES), jnp.float32),
+            pltpu.VMEM((2, n_dev, LANES), jnp.float32),
+            pltpu.VMEM((2, 2, 16, LANES), jnp.float32),
+            pltpu.VMEM((1, width), jnp.float32),
+            own_part,
+            own_part,
+            own_part,
+            cross_part,
+            cross_part,
+            own_part,
+            pltpu.VMEM((2, rows + TILE, LANES), jnp.float32),
+            chunk_sems,
+            chunk_sems,
+            chunk_sems,
+            pair_sems,
+            pair_sems,
+        ]
+        + [plane_sems] * 8,
+        compiler_params=pltpu.CompilerParams(
+            collective_id=0, has_side_effects=True, vmem_limit_bytes=48 * 1024 * 1024
+        ),
+    )(view_a, view_b)
+    return (grad_a, grad_b, loss[0, 0])
+
+
 def solution(mesh):
     in_specs = (P("dp", ("row", "col")), P("dp", ("row", "col")))
     out_specs = (P("dp", ("row", "col")), P("dp", ("row", "col")), P())

time: 239 us -> 45.3 us (0.19)
  waiting for transfers between devices: 163 us -> 0 us
  Pallas kernels: 0 us -> 39.9 us
  blocking collectives: 39.2 us -> 0 us
  between operations: 17.9 us -> 0.65 us
  other arithmetic: 12.9 us -> 0 us
  matrix products: 5.1 us -> 0 us
  local copies, waits for them, and re-layouts: 0.09 us -> 4.53 us
    psum x1 -> x0, waiting for transfers between devices: 127 us -> none  [on_device(): gram, local = lax.psum((gram, local), ('dp', 'row', 'col'))]
    pallas_call x0 -> x1, Pallas kernels: none -> 39.9 us  [on_device(): pl.pallas_call(functools.partial(gram_kernel, n_row, n_col), out_shape=(g...]
    psum x1 -> x0, blocking collectives: 39.2 us -> none  [on_device(): gram, local = lax.psum((gram, local), ('dp', 'row', 'col'))]
    all_gather x1 -> x0, waiting for transfers between devices: 36.3 us -> none  [on_device(): full = lax.all_gather(own, 'dp', axis=1, tiled=True).astype(jnp.float32)]
    reduce_sum x4 -> x0, other arithmetic: 5.45 us -> none  [the longest x1 2.13 us: on_device(): mean = jnp.sum(full, axis=1, keepdims=True) / total]
    dot_general x2 -> x0, matrix products: 5.1 us -> none  [the longest x1 3.84 us: on_device(): lax.dot_general(lean, cent32, (((2,), (1,)), ((0,), (0,))), preferred_ele...]
    convert_element_type x2 -> x0, other arithmetic: 4.93 us -> none  [the longest x1 2.56 us: on_device(): cent32 = cent.astype(jnp.float32)]
    unnamed x8 -> x6, local copies, waits for them, and re-layouts: 0.09 us -> 4.01 us
  transfers between devices with their start and end apart: 2 -> 0, of which waited for: 2 -> 0; matrix products, arithmetic and copies ran while one was open for 0% -> 0% of each run, Pallas kernels for 0% -> 0%
where the time goes in v3:
time: 45.3 us; the launch traced here: 45.1 us
  Pallas kernels  39.9 us (88%)
  local copies, waits for them, and re-layouts  4.53 us (10%)
  between operations  0.65 us (1%)
    pallas_call x1, Pallas kernels, on_device(): pl.pallas_call(functools.partial(gram_kernel, n_row, n_col), out_shape=(g...  39.9 us
    unnamed x6, local copies, waits for them, and re-layouts  4.01 us

profile of v3, /device:TPU:0, one launch (start us, length us, event | category | flops | bytes accessed | tf_op | source)
XLA Modules:
  0.0 45.1 jit_solution(10354691753951165352)
XLA Ops:
  0.6 0.0 copy-start
  0.6 1.0 %copy-done = bf16[128,2048]{1,0:T(8,128)(2,1)S(1)} copy-done((bf16[128,2048]{1,0:T(8,128)(2,1)S(1)}, bf16[128,2048]{1,0:T(8,128)(2,1)}, u32[]{:S(2)}) %copy-start) | copy-done | bytes 524312
  1.7 0.0 copy-start.1
  1.7 1.0 %copy-done.1 = bf16[128,2048]{1,0:T(8,128)(2,1)S(1)} copy-done((bf16[128,2048]{1,0:T(8,128)(2,1)S(1)}, bf16[128,2048]{1,0:T(8,128)(2,1)}, u32[]{:S(2)}) %copy-start.1) | copy-done | bytes 524312
  2.7 39.9 %shard_map.49 = (f32[128,2048]{1,0:T(8,128)S(1)}, f32[128,2048]{1,0:T(8,128)S(1)}, f32[8,128]{1,0:T(8,128)S(1)}) custom-call(bf16[128,2048]{1,0:T(8,128)(2,1)S(1)} %copy-done, bf16[128,2048]{1,0:T(8,128)(2,1)S(1)} %copy-done.1), custom_call_target="tpu_custom_call" | custom-call | tf_op jit(solution)/shard_map/pallas_call | solution.py:392
  42.7 0.5 %slice.3 = f32[1,1]{1,0:T(1,128)} slice(f32[8,128]{1,0:T(8,128)S(1)} %get-tuple-element.8), slice={[0:1], [0:1]} | slice | bytes 8 | tf_op jit(solution)/shard_map/slice | solution.py:425
  43.2 1.0 %copy.7 = f32[128,2048]{1,0:T(8,128)} copy(f32[128,2048]{1,0:T(8,128)S(1)} %get-tuple-element.12) | data formatting | bytes 2097152
  44.1 1.0 %copy.8 = f32[128,2048]{1,0:T(8,128)} copy(f32[128,2048]{1,0:T(8,128)S(1)} %get-tuple-element.13) | data formatting | bytes 2097152
Async XLA Ops:
  0.6 1.0 %copy-start = (bf16[128,2048]{1,0:T(8,128)(2,1)S(1)}, bf16[128,2048]{1,0:T(8,128)(2,1)}, u32[]{:S(2)}) copy-start(bf16[128,2048]{1,0:T(8,128)(2,1)} %view_a.1) | copy-start | bytes 1572868
  1.7 1.0 %copy-start.1 = (bf16[128,2048]{1,0:T(8,128)(2,1)S(1)}, bf16[128,2048]{1,0:T(8,128)(2,1)}, u32[]{:S(2)}) copy-start(bf16[128,2048]{1,0:T(8,128)(2,1)} %view_b.1) | copy-start | bytes 1572868

commit v4 on v3

--- a/solution.py
+++ b/solution.py
@@ -107,6 +107,7 @@
     coef = 2.0 * total / (25.0 * (total - 1))
     n_chunks = other.shape[0]
     half = n_chunks // 2
+    held = 2
     width = other.shape[3]
     rows = all_own.shape[1]
     dp = lax.axis_index("dp")
@@ -174,7 +175,7 @@
     lax.fori_loop(0, n_chunks, own_sums, 0)
     sums_copy = to_partner(sums.at[0], sums.at[1], sums_sem.at[0], sums_sem.at[1])
     sums_copy.start()
-    lax.fori_loop(1, n_chunks, send_views, 0)
+    lax.fori_loop(1, n_chunks - held, send_views, 0)
     gram_own[...] = jnp.zeros_like(gram_own)
     gram_cross[...] = jnp.zeros_like(gram_cross)
     extra[...] = jnp.zeros_like(extra)
@@ -289,12 +290,18 @@
             squares = add_rows(gap * gap) + add_rows(gap_other * gap_other)
             local[...] += 25.0 * squares / (total * f_all)
 
-    take_chunk(0, True)
+    def take_chunks(first, last, multiply):
+        def one(k, carry):
+            take_chunk(k, multiply)
+            return carry
+
+        lax.fori_loop(first, last, one, 0)
+
+    take_chunks(0, 1, True)
     end_own()
     all_own[me] = added(in_own)
     start_own_all()
-    for k in range(1, half):
-        take_chunk(k, True)
+    take_chunks(1, half, True)
 
     local_sum = jnp.broadcast_to(jnp.sum(local[...]).reshape(1, 1), (1, LANES))
     tail = jnp.concatenate(
@@ -317,19 +324,21 @@
         return jnp.broadcast_to(jnp.sum(square).reshape(1, 1), (1, LANES))
 
     own_square = squared(all_own)
+    take_chunks(half, half + 1, False)
     end_cross()
     piece = added(in_cross)
     pair[0] = piece
     pair[0, rows + 5:rows + 6, :] = own_square
     pair_copy = to_partner(pair.at[0], pair.at[1], pair_sem.at[0], pair_sem.at[1])
     pair_copy.start()
-    for k in range(half, n_chunks - 1):
-        take_chunk(k, False)
+    lax.fori_loop(n_chunks - held, n_chunks, send_views, 0)
+    take_chunks(half + 1, n_chunks - held, False)
     pair_copy.wait()
     piece = pair[0] + pair[1]
     all_cross[me] = piece[0:rows, :]
     start_cross_all()
     tail = piece[rows:rows + TILE, :]
+    take_chunks(n_chunks - held, n_chunks - 1, False)
     end_cross_all()
 
     first_half = jnp.full((n_dev, LANES), dp, jnp.int32) == 0
@@ -358,9 +367,9 @@
     lax.fori_loop(0, n_chunks - 1, give_chunk, 0)
     square = tail[5:6, :] + 2.0 * squared(all_cross)
     loss = tail[4:5, :] + square / (float(total - 1) * float(total - 1) * f_all)
-    loss_out[...] = jnp.broadcast_to(loss * (total / (50.0 * f_all)), (TILE, LANES))
-    take_chunk(n_chunks - 1, False)
-    give_chunk(n_chunks - 1, 0)
+    loss_out[...] = loss[0:1, 0:1] * (total / (50.0 * f_all))
+    take_chunks(n_chunks - 1, n_chunks, False)
+    lax.fori_loop(n_chunks - 1, n_chunks, give_chunk, 0)
 
     def end_views(c, carry):
         view_copy(0, c).wait_send()
@@ -377,7 +386,7 @@
     n_dev, shard = view_a.shape
     total = 2 * n_dev
     rows = total // n_plane
-    n_chunks = 4
+    n_chunks = 8
     width = shard // n_chunks
     fits = n_dev == LANES and rows > 0 and rows % TILE == 0 and n_dev % rows == 0
     if lax.axis_size("dp") != 2 or not fits or shard % (n_chunks * LANES):
@@ -391,8 +400,8 @@
     pair_sems = pltpu.SemaphoreType.DMA((2,))
     grad_a, grad_b, loss = pl.pallas_call(
         functools.partial(gram_kernel, n_row, n_col),
-        out_shape=(grad, grad, jax.ShapeDtypeStruct((TILE, LANES), jnp.float32)),
-        in_specs=[pl.BlockSpec(memory_space=pl.ANY)] * 2,
+        out_shape=(grad, grad, jax.ShapeDtypeStruct((1, 1), jnp.float32)),
+        in_specs=[pl.BlockSpec(memory_space=pltpu.HBM)] * 2,
         out_specs=(space,) * 3,
         scratch_shapes=[
             pltpu.VMEM((2, n_dev, shard), jnp.bfloat16),
@@ -422,7 +431,7 @@
             collective_id=0, has_side_effects=True, vmem_limit_bytes=48 * 1024 * 1024
         ),
     )(view_a, view_b)
-    return (grad_a, grad_b, loss[0, 0])
+    return (grad_a, grad_b, loss.reshape(()))
 
 
 def solution(mesh):

time: 45.3 us -> 45.8 us (1.011)
  between operations: 0.65 us -> 2.41 us
  Pallas kernels: 39.9 us -> 39.1 us
  local copies, waits for them, and re-layouts: 4.53 us -> 4.02 us
    pallas_call x1, Pallas kernels: 39.9 us -> 39.1 us  [on_device(): pl.pallas_call(functools.partial(gram_kernel, n_row, n_col), out_shape=(g...]
    slice x1 -> x0, local copies, waits for them, and re-layouts: 0.51 us -> none  [on_device(): return (grad_a, grad_b, loss[0, 0])]
where the time goes in v4:
time: 45.8 us; the launch traced here: 45.5 us
  Pallas kernels  39.1 us (85%)
  local copies, waits for them, and re-layouts  4.02 us (9%)
  between operations  2.41 us (5%)
    pallas_call x1, Pallas kernels, on_device(): pl.pallas_call(functools.partial(gram_kernel, n_row, n_col), out_shape=(g...  39.1 us
    unnamed x6, local copies, waits for them, and re-layouts  4.02 us

profile of v4, /device:TPU:0, one launch (start us, length us, event | category | flops | bytes accessed | tf_op | source)
XLA Modules:
  0.0 45.5 jit_solution(17712492166545685142)
XLA Ops:
  0.6 0.0 copy-start
  0.6 1.0 %copy-done = bf16[128,2048]{1,0:T(8,128)(2,1)S(1)} copy-done((bf16[128,2048]{1,0:T(8,128)(2,1)S(1)}, bf16[128,2048]{1,0:T(8,128)(2,1)}, u32[]{:S(2)}) %copy-start) | copy-done | bytes 524312
  1.7 0.0 copy-start.1
  1.7 1.0 %copy-done.1 = bf16[128,2048]{1,0:T(8,128)(2,1)S(1)} copy-done((bf16[128,2048]{1,0:T(8,128)(2,1)S(1)}, bf16[128,2048]{1,0:T(8,128)(2,1)}, u32[]{:S(2)}) %copy-start.1) | copy-done | bytes 524312
  2.7 39.1 %shard_map.49 = (f32[128,2048]{1,0:T(8,128)S(1)}, f32[128,2048]{1,0:T(8,128)S(1)}, f32[1,1]{1,0:T(1,128)}) custom-call(bf16[128,2048]{1,0:T(8,128)(2,1)S(1)} %copy-done, bf16[128,2048]{1,0:T(8,128)(2,1)S(1)} %copy-done.1), custom_call_target="tpu_custom_call" | custom-call | tf_op jit(solution)/shard_map/pallas_call | solution.py:401
  41.8 1.0 %copy.8 = f32[128,2048]{1,0:T(8,128)} copy(f32[128,2048]{1,0:T(8,128)S(1)} %get-tuple-element.12) | data formatting | bytes 2097152
  42.8 1.0 %copy.9 = f32[128,2048]{1,0:T(8,128)} copy(f32[128,2048]{1,0:T(8,128)S(1)} %get-tuple-element.13) | data formatting | bytes 2097152
Async XLA Ops:
  0.6 1.0 %copy-start = (bf16[128,2048]{1,0:T(8,128)(2,1)S(1)}, bf16[128,2048]{1,0:T(8,128)(2,1)}, u32[]{:S(2)}) copy-start(bf16[128,2048]{1,0:T(8,128)(2,1)} %view_a.1) | copy-start | bytes 1572868
  1.7 1.0 %copy-start.1 = (bf16[128,2048]{1,0:T(8,128)(2,1)S(1)}, bf16[128,2048]{1,0:T(8,128)(2,1)}, u32[]{:S(2)}) copy-start(bf16[128,2048]{1,0:T(8,128)(2,1)} %view_b.1) | copy-start | bytes 1572868

commit v5 on v4

--- a/solution.py
+++ b/solution.py
@@ -75,7 +75,6 @@
     sums,
     gram_own,
     gram_cross,
-    extra,
     local,
     out_own,
     in_own,
@@ -83,6 +82,7 @@
     out_cross,
     in_cross,
     all_cross,
+    all_tail,
     pair,
     load_sem,
     view_send,
@@ -97,6 +97,8 @@
     cross_recv,
     cross_all_send,
     cross_all_recv,
+    tail_send,
+    tail_recv,
 ):
     views = (view_a, view_b)
     grads = (grad_a, grad_b)
@@ -178,7 +180,6 @@
     lax.fori_loop(1, n_chunks - held, send_views, 0)
     gram_own[...] = jnp.zeros_like(gram_own)
     gram_cross[...] = jnp.zeros_like(gram_cross)
-    extra[...] = jnp.zeros_like(extra)
     local[...] = jnp.zeros_like(local)
     sums_copy.wait()
     dims = (((1,), (1,)), ((), ()))
@@ -241,6 +242,7 @@
     start_cross_all, end_cross_all = exchange(
         all_cross, all_cross, cross_all_send, cross_all_recv, False
     )
+    start_tail, end_tail = exchange(all_tail, all_tail, tail_send, tail_recv, False)
     per_block = n_dev // rows
     for r in range(n_plane):
         first = r % per_block * rows
@@ -269,22 +271,12 @@
             grads[v][:, cols] = (gap if v == 0 else -gap) - rest
             if multiply:
                 local[...] += (25.0 * jnp.maximum(1.0 - std, 0.0) - diag * diag) / f_all
-                high = column.astype(jnp.bfloat16).astype(jnp.float32)
-                row = lax.broadcasted_iota(jnp.int32, (16, width), 0)
-                parts = jnp.where(row == 0, high, jnp.where(row == 1, column - high, 0.0))
                 gram_cross[v] += lax.dot_general(
                     cent[v, 0, :, cols],
                     cent[v, 1, :, cols],
                     dims,
                     preferred_element_type=jnp.float32,
                 )
-                for h in range(2):
-                    extra[v, h] += lax.dot_general(
-                        parts.astype(jnp.bfloat16),
-                        cent[v, h, :, cols],
-                        dims,
-                        preferred_element_type=jnp.float32,
-                    )
         if multiply:
             gap_other = other[c, 0].astype(jnp.float32) - other[c, 1].astype(jnp.float32)
             squares = add_rows(gap * gap) + add_rows(gap_other * gap_other)
@@ -303,16 +295,9 @@
     start_own_all()
     take_chunks(1, half, True)
 
-    local_sum = jnp.broadcast_to(jnp.sum(local[...]).reshape(1, 1), (1, LANES))
-    tail = jnp.concatenate(
-        [add_rows(extra[v, h]) for v in range(2) for h in range(2)]
-        + [local_sum, jnp.zeros((TILE - 5, LANES), jnp.float32)],
-        axis=0,
-    )
     for r in range(n_plane):
         first = r % per_block * rows
-        out_cross[r, 0:rows, :] = gram_cross[r // per_block, first:first + rows, :]
-        out_cross[r, rows:rows + TILE, :] = tail
+        out_cross[r] = gram_cross[r // per_block, first:first + rows, :]
     start_cross()
     in_cross[me] = out_cross[me]
     end_own_all()
@@ -323,12 +308,22 @@
             square = square + ref[r] * ref[r]
         return jnp.broadcast_to(jnp.sum(square).reshape(1, 1), (1, LANES))
 
-    own_square = squared(all_own)
+    def whole(ref, v):
+        return jnp.concatenate([ref[v * per_block + q] for q in range(per_block)], axis=0)
+
+    pair[0, rows:rows + TILE, :] = jnp.concatenate(
+        [
+            add_rows(whole(all_own, 0)),
+            add_rows(whole(all_own, 1)),
+            jnp.broadcast_to(jnp.sum(local[...]).reshape(1, 1), (1, LANES)),
+            squared(all_own),
+            jnp.zeros((TILE - 4, LANES), jnp.float32),
+        ],
+        axis=0,
+    )
     take_chunks(half, half + 1, False)
     end_cross()
-    piece = added(in_cross)
-    pair[0] = piece
-    pair[0, rows + 5:rows + 6, :] = own_square
+    pair[0, 0:rows, :] = added(in_cross)
     pair_copy = to_partner(pair.at[0], pair.at[1], pair_sem.at[0], pair_sem.at[1])
     pair_copy.start()
     lax.fori_loop(n_chunks - held, n_chunks, send_views, 0)
@@ -336,19 +331,24 @@
     pair_copy.wait()
     piece = pair[0] + pair[1]
     all_cross[me] = piece[0:rows, :]
+    all_tail[me] = piece[rows:rows + TILE, :]
     start_cross_all()
-    tail = piece[rows:rows + TILE, :]
+    start_tail()
     take_chunks(n_chunks - held, n_chunks - 1, False)
     end_cross_all()
 
     first_half = jnp.full((n_dev, LANES), dp, jnp.int32) == 0
     factors = []
     for v in range(2):
-        span = range(v * per_block, (v + 1) * per_block)
-        own = jnp.concatenate([all_own[r] for r in span], axis=0)
-        cross = jnp.concatenate([all_cross[r] for r in span], axis=0)
-        left = jnp.where(first_half, own, cross.T) - tail[2 * v:2 * v + 1, :] / total
-        right = jnp.where(first_half, cross, own) - tail[2 * v + 1:2 * v + 2, :] / total
+        own = whole(all_own, v)
+        cross = whole(all_cross, v)
+        flipped = cross.T
+        rest = jnp.where(first_half, flipped, cross)
+        own = own - (add_rows(own) + add_rows(rest)) / total
+        rest = jnp.where(first_half, cross, flipped)
+        rest = rest - (add_rows(rest) + pair[1, rows + v:rows + v + 1, :]) / total
+        left = jnp.where(first_half, own, rest)
+        right = jnp.where(first_half, rest, own)
         factor = jnp.concatenate([left, right], axis=1) * (coef / (total - 1))
         one = factor.astype(jnp.bfloat16)
         rest = factor - one.astype(jnp.float32)
@@ -365,11 +365,13 @@
         return carry
 
     lax.fori_loop(0, n_chunks - 1, give_chunk, 0)
-    square = tail[5:6, :] + 2.0 * squared(all_cross)
-    loss = tail[4:5, :] + square / (float(total - 1) * float(total - 1) * f_all)
-    loss_out[...] = loss[0:1, 0:1] * (total / (50.0 * f_all))
     take_chunks(n_chunks - 1, n_chunks, False)
     lax.fori_loop(n_chunks - 1, n_chunks, give_chunk, 0)
+
+    end_tail()
+    square = all_tail[me][3:4, :] + 2.0 * squared(all_cross)
+    loss = added(all_tail)[2:3, :] + square / (float(total - 1) * float(total - 1) * f_all)
+    loss_out[...] = loss[0:1, 0:1] * (total / (50.0 * f_all))
 
     def end_views(c, carry):
         view_copy(0, c).wait_send()
@@ -393,8 +395,9 @@
         return plain(view_a, view_b)
     space = pl.BlockSpec(memory_space=pltpu.VMEM)
     grad = jax.ShapeDtypeStruct((n_dev, shard), jnp.float32)
+    view_a = pltpu.with_memory_space_constraint(view_a, pltpu.HBM)
+    view_b = pltpu.with_memory_space_constraint(view_b, pltpu.HBM)
     own_part = pltpu.VMEM((n_plane, rows, LANES), jnp.float32)
-    cross_part = pltpu.VMEM((n_plane, rows + TILE, LANES), jnp.float32)
     plane_sems = pltpu.SemaphoreType.DMA((n_plane,))
     chunk_sems = pltpu.SemaphoreType.DMA((n_chunks, 2))
     pair_sems = pltpu.SemaphoreType.DMA((2,))
@@ -411,14 +414,14 @@
             pltpu.VMEM((2, 2, shard), jnp.float32),
             pltpu.VMEM((2, n_dev, LANES), jnp.float32),
             pltpu.VMEM((2, n_dev, LANES), jnp.float32),
-            pltpu.VMEM((2, 2, 16, LANES), jnp.float32),
             pltpu.VMEM((1, width), jnp.float32),
             own_part,
             own_part,
             own_part,
-            cross_part,
-            cross_part,
-            own_part,
+            own_part,
+            own_part,
+            own_part,
+            pltpu.VMEM((n_plane, TILE, LANES), jnp.float32),
             pltpu.VMEM((2, rows + TILE, LANES), jnp.float32),
             chunk_sems,
             chunk_sems,
@@ -426,7 +429,7 @@
             pair_sems,
             pair_sems,
         ]
-        + [plane_sems] * 8,
+        + [plane_sems] * 10,
         compiler_params=pltpu.CompilerParams(
             collective_id=0, has_side_effects=True, vmem_limit_bytes=48 * 1024 * 1024
         ),

time: 45.8 us -> 42.8 us (0.934)
  local copies, waits for them, and re-layouts: 4.02 us -> 1.94 us
  Pallas kernels: 39.1 us -> 38.4 us
    unnamed x6 -> x2, local copies, waits for them, and re-layouts: 4.02 us -> 1.94 us
    pallas_call x1, Pallas kernels: 39.1 us -> 38.4 us  [on_device(): pl.pallas_call(functools.partial(gram_kernel, n_row, n_col), out_shape=(g...]
where the time goes in v5:
time: 42.8 us; the launch traced here: 42.7 us
  Pallas kernels  38.4 us (90%)
  between operations  2.33 us (5%)
  local copies, waits for them, and re-layouts  1.94 us (5%)
    pallas_call x1, Pallas kernels, on_device(): pl.pallas_call(functools.partial(gram_kernel, n_row, n_col), out_shape=(g...  38.4 us
    unnamed x2, local copies, waits for them, and re-layouts  1.94 us

profile of v5, /device:TPU:0, one launch (start us, length us, event | category | flops | bytes accessed | tf_op | source)
XLA Modules:
  0.0 42.7 jit_solution(11136138668116424178)
XLA Ops:
  0.6 38.4 %shard_map.49 = (f32[128,2048]{1,0:T(8,128)S(1)}, f32[128,2048]{1,0:T(8,128)S(1)}, f32[1,1]{1,0:T(1,128)}) custom-call(bf16[128,2048]{1,0:T(8,128)(2,1)} %view_a.1, bf16[128,2048]{1,0:T(8,128)(2,1)} %view_b.1), custom_call_target="tpu_custom_call" | custom-call | tf_op jit(solution)/shard_map/pallas_call | solution.py:404
  39.0 1.0 %copy.8 = f32[128,2048]{1,0:T(8,128)} copy(f32[128,2048]{1,0:T(8,128)S(1)} %get-tuple-element.12) | data formatting | bytes 2097152
  40.0 1.0 %copy.9 = f32[128,2048]{1,0:T(8,128)} copy(f32[128,2048]{1,0:T(8,128)S(1)} %get-tuple-element.13) | data formatting | bytes 2097152

commit v6 on v5

--- a/solution.py
+++ b/solution.py
@@ -177,7 +177,7 @@
     lax.fori_loop(0, n_chunks, own_sums, 0)
     sums_copy = to_partner(sums.at[0], sums.at[1], sums_sem.at[0], sums_sem.at[1])
     sums_copy.start()
-    lax.fori_loop(1, n_chunks - held, send_views, 0)
+    lax.fori_loop(1, 2, send_views, 0)
     gram_own[...] = jnp.zeros_like(gram_own)
     gram_cross[...] = jnp.zeros_like(gram_cross)
     local[...] = jnp.zeros_like(local)
@@ -199,7 +199,9 @@
             gram_own[v] += lax.dot_general(kept, kept, dims, preferred_element_type=jnp.float32)
         return carry
 
-    lax.fori_loop(0, n_chunks, center_own, 0)
+    lax.fori_loop(0, half, center_own, 0)
+    lax.fori_loop(2, 3, send_views, 0)
+    lax.fori_loop(half, n_chunks, center_own, 0)
 
     def exchange(source, target, send_sem, recv_sem, scatter):
         def copy(peer, slot):
@@ -290,10 +292,14 @@
         lax.fori_loop(first, last, one, 0)
 
     take_chunks(0, 1, True)
+    lax.fori_loop(3, half, send_views, 0)
     end_own()
     all_own[me] = added(in_own)
     start_own_all()
-    take_chunks(1, half, True)
+    take_chunks(1, half - 1, True)
+    lax.fori_loop(half, half + 1, send_views, 0)
+    take_chunks(half - 1, half, True)
+    lax.fori_loop(half + 1, n_chunks - held, send_views, 0)
 
     for r in range(n_plane):
         first = r % per_block * rows

time: 42.8 us -> 43.4 us (1.014)
  Pallas kernels: 38.4 us -> 39 us
    pallas_call x1, Pallas kernels: 38.4 us -> 39 us  [on_device(): pl.pallas_call(functools.partial(gram_kernel, n_row, n_col), out_shape=(g...]
where the time goes in v6:
time: 43.4 us; the launch traced here: 43.2 us
  Pallas kernels  39 us (90%)
  between operations  2.33 us (5%)
  local copies, waits for them, and re-layouts  1.94 us (4%)
    pallas_call x1, Pallas kernels, on_device(): pl.pallas_call(functools.partial(gram_kernel, n_row, n_col), out_shape=(g...  39 us
    unnamed x2, local copies, waits for them, and re-layouts  1.94 us

profile of v6, /device:TPU:0, one launch (start us, length us, event | category | flops | bytes accessed | tf_op | source)
XLA Modules:
  0.0 43.2 jit_solution(3830595902725453181)
XLA Ops:
  0.6 39.0 %shard_map.49 = (f32[128,2048]{1,0:T(8,128)S(1)}, f32[128,2048]{1,0:T(8,128)S(1)}, f32[1,1]{1,0:T(1,128)}) custom-call(bf16[128,2048]{1,0:T(8,128)(2,1)} %view_a.1, bf16[128,2048]{1,0:T(8,128)(2,1)} %view_b.1), custom_call_target="tpu_custom_call" | custom-call | tf_op jit(solution)/shard_map/pallas_call | solution.py:410
  39.6 1.0 %copy.8 = f32[128,2048]{1,0:T(8,128)} copy(f32[128,2048]{1,0:T(8,128)S(1)} %get-tuple-element.12) | data formatting | bytes 2097152
  40.6 1.0 %copy.9 = f32[128,2048]{1,0:T(8,128)} copy(f32[128,2048]{1,0:T(8,128)S(1)} %get-tuple-element.13) | data formatting | bytes 2097152
